TPU v7x, 32 devices: a whole 2x2x4 slice. The times are simulated.
32 devices in a mesh: seg: 8 (over y, x, core), fft: 4 (over z).
Axes of the slice: x: 2, y: 2, z: 4, core: 2. Of those that a mesh axis runs over, the one named last changes fastest.
Arguments:
- voltage: float32 [8, 2, 256, 4096], P('seg', None, None, 'fft'), may hold values from -6 to 6
- chirp_phase: float32 [2, 512, 4096], P(None, 'fft'), may hold values from -3.140625 to 3.140625
Outputs:
- dedispersed: float32 [8, 2, 256, 4096], P('seg', None, None, 'fft')
All inputs are finite; a program needn't handle non-finite values.
Results may differ from a plain program's by a relative error of at most 0.0001.
Values sent between devices are 32-bit elements; how exact they have to be, the bound alone decides.
No kernel may reach another device: no remote copies, remote signals or barrier semaphores. Data moves between devices by JAX's collectives and lax.ppermute only.
A program may use at most 128 MiB of HBM per device.

v0:
```python
import math

import jax
import jax.numpy as jnp
from jax import lax
from jax.sharding import PartitionSpec as P

B1 = 64


HIGHEST = lax.Precision.HIGHEST


def passed_along(shard, axis, by):
    length = lax.axis_size(axis)
    pairs = [(i, i + by) for i in range(length) if 0 <= i + by < length]
    return lax.ppermute(shard, axis, pairs)


def rotation(products, period):
    reduced = jnp.mod(products, period).astype(jnp.float32)
    angles = reduced * jnp.float32(-2.0 * math.pi / period)
    return jnp.stack([jnp.cos(angles), jnp.sin(angles)])


def conjugate(pair):
    return jnp.stack([pair[0], -pair[1]])


def real_table(pair):
    return jnp.stack([jnp.stack([pair[0], pair[1]]), jnp.stack([-pair[1], pair[0]])])


def complex_mul(left_pair, right_pair):
    first = left_pair[0] * right_pair[0] - left_pair[1] * right_pair[1]
    second = left_pair[0] * right_pair[1] + left_pair[1] * right_pair[0]
    return jnp.stack([first, second])


def fold_order(row_count, groups):
    half_count = row_count // (2 * groups)
    places = jnp.arange(row_count, dtype=jnp.int32)
    within = places % (2 * half_count)
    base_row = places // (2 * half_count) * half_count + within % half_count
    mirror_row = jnp.where(base_row > 0, row_count - base_row, row_count // 2)
    return jnp.where(within >= half_count, mirror_row, base_row)


def mirrored(values, half_count, is_first):
    swapped = jnp.concatenate([values[:, half_count:], values[:, :half_count]], axis=1)
    flipped = jnp.flip(swapped, axis=2)
    zero_row = jnp.roll(jnp.flip(values[:, 0], axis=1), 1, axis=1)
    middle_row = jnp.flip(values[:, half_count], axis=1)
    flipped = flipped.at[:, 0].set(jnp.where(is_first, zero_row, flipped[:, 0]))
    return flipped.at[:, half_count].set(jnp.where(is_first, middle_row, flipped[:, half_count]))


def per_device(voltage, chirp_phase):
    groups = lax.axis_size("fft")
    device = lax.axis_index("fft")
    quarter = voltage.shape[2]
    row_count = 4 * quarter
    local_width = voltage.shape[3]
    columns = local_width * groups
    second_len = columns // B1
    total_bins = row_count * columns
    half_count = row_count // (2 * groups)
    local_rows = 2 * half_count
    is_first = device == 0
    row_order = fold_order(row_count, groups)
    local_order = lax.dynamic_slice_in_dim(row_order, device * local_rows, local_rows)
    first_range = jnp.arange(B1, dtype=jnp.int32)
    second_range = jnp.arange(second_len, dtype=jnp.int32)
    column_range = jnp.arange(columns, dtype=jnp.int32)
    sample_rows = jnp.arange(quarter, dtype=jnp.int32)
    entry_table = real_table(rotation(sample_rows[:, None] * row_order[None, :], row_count))
    spread = jnp.einsum("pmb,pqmr->qrb", voltage[0], entry_table, precision=HIGHEST)
    local_columns = device * local_width + jnp.arange(local_width, dtype=jnp.int32)
    spread = complex_mul(spread, rotation(row_order[:, None] * local_columns[None, :], total_bins))
    spread = spread.reshape(2, row_count, B1 // groups, second_len)
    section_one = rotation(first_range[:, None] * first_range[None, :], B1)
    section_two = rotation(second_range[:, None] * second_range[None, :], second_len)
    block_turn = rotation(first_range[:, None] * second_range[None, :], columns)
    forward_one = real_table(section_one)
    forward_two = real_table(section_two)
    gathered = jnp.einsum(
        "prun,pquk->qrkn",
        lax.all_to_all(spread, "fft", split_axis=1, concat_axis=2, tiled=True),
        forward_one,
        precision=HIGHEST,
    )
    gathered = complex_mul(gathered, block_turn)
    spectrum = jnp.einsum("prkv,pqvj->qrjk", gathered, forward_two, precision=HIGHEST)
    spectrum = spectrum.reshape(2, local_rows, columns)
    bins = local_order[:, None] + row_count * column_range[None, :]
    bin_turn = rotation(bins, 2 * total_bins)
    partner = conjugate(mirrored(spectrum, half_count, is_first))
    even_spec = 0.5 * (spectrum + partner)
    odd_spec = jnp.stack([0.5 * (spectrum[1] - partner[1]), -0.5 * (spectrum[0] - partner[0])])
    transformed = even_spec + complex_mul(odd_spec, bin_turn)
    phase_rows = chirp_phase.reshape(local_rows, columns)
    filtered = complex_mul(transformed, jnp.stack([jnp.cos(phase_rows), jnp.sin(phase_rows)]))
    live_bins = bins > 0
    filtered = jnp.where(live_bins[None], filtered, 0.0)
    partner = conjugate(mirrored(filtered, half_count, is_first))
    even_back = 0.5 * (filtered + partner)
    odd_back = complex_mul(0.5 * (filtered - partner), conjugate(bin_turn))
    packed = jnp.stack([even_back[0] - odd_back[1], even_back[1] + odd_back[0]])
    packed = packed.reshape(2, local_rows, second_len, B1)
    packed = jnp.einsum(
        "prjk,pqjv->qrkv", packed, real_table(conjugate(section_two)), precision=HIGHEST
    )
    packed = complex_mul(packed, conjugate(block_turn))
    packed = jnp.einsum(
        "prkv,pqku->qruv", packed, real_table(conjugate(section_one)), precision=HIGHEST
    )
    packed = packed.reshape(2, local_rows, columns)
    packed = complex_mul(
        packed, conjugate(rotation(local_order[:, None] * column_range[None, :], total_bins))
    )
    packed = packed.reshape(2, local_rows, groups, local_width)
    exit_turn = rotation(
        row_order[:, None] * jnp.arange(row_count, dtype=jnp.int32)[None, :], row_count
    )
    exit_table = real_table(jnp.stack([exit_turn[0] / total_bins, -exit_turn[1] / total_bins]))
    signal = jnp.einsum(
        "pron,pqrm->qmon",
        lax.all_to_all(packed, "fft", split_axis=2, concat_axis=1, tiled=True),
        exit_table,
        precision=HIGHEST,
    )
    samples = signal.reshape(2, row_count, local_width)

    def sample_block(block_id):
        lower = block_id * quarter
        return samples[:, lower : lower + quarter]

    running = sample_block(3)
    for block_id in (2, 1, 0):
        running = sample_block(block_id) + passed_along(running, "seg", 1)
    return running[None]


def solution(mesh):
    in_specs = (P("seg", None, None, "fft"), P(None, "fft", None))
    out_specs = P("seg", None, None, "fft")
    return jax.shard_map(
        per_device, mesh=mesh, in_specs=in_specs, out_specs=out_specs, check_vma=False
    )
```

profile of v0, /device:TPU:1, one launch (start us, length us, event | category | flops | bytes accessed | tf_op | source)
XLA Modules:
  0.0 1189.1 jit_solution(14058649215511448088)
XLA Ops:
  4.6 15.0 %fusion.38 = f32[2,1024,1024]{1,2,0:T(8,128)S(1)} fusion(f32[1,2,256,1024]{3,2,0,1:T(8,128)S(1)} %get-tuple-element.92, f32[1,2,256,1024]{3,2,0,1:T(8,128)S(1)} %get-tuple-element.91, f32[1,2,256,1024]{3,2,1,0:T(8,128)S(1)} %copy-done), kind=kOutput, calls=%fused_computation.101 | convolution fusion | flops 12885950464 | bytes 14680064 | tf_op jit(solution)/shard_map/pmb,pqmr->qrb/dot_general | solution.py:77
  19.7 36.3 %negate_multiply_fusion = (f32[1,1024,1024]{1,2,0:T(8,128)}, f32[1,1024,1024]{1,2,0:T(8,128)}, f32[1,1024,1024]{1,2,0:T(8,128)}, f32[1,1024,1024]{1,2,0:T(8,128)}, f32[1,1024,1024]{1,2,0:T(8,128)}) fusion(s32[1024]{0:T(1024)S(1)} %get-tuple-element.108, f32[2,1024,1024]{1,2,0:T(8,128)S(1)} %fusion.38, s32[1024]{0:T(1024)S(1)} %get-tuple-element.107), kind=kLoop, calls=%fused_computation.96 | loop fusion | flops 39845888 | bytes 29368320 | tf_op jit(solution)/shard_map/div | solution.py:125
  72.2 11.6 fusion.114
  83.8 14.4 %reshape.1130 = f32[4,1,524288]{2,1,0:T(1,128)} reshape(f32[1024,2,16,64]{3,2,1,0:T(8,128)} %fusion.114) | data formatting | bytes 16777216
  104.1 16.7 %fusion.113 = (f32[2,128,4096]{2,1,0:T(8,128)}, f32[2,128,4096]{2,1,0:T(8,128)}) fusion(f32[2,128,4096]{2,1,0:T(8,128)} %param.11), kind=kLoop, calls=%fused_computation.204 | loop fusion | bytes 12582912 | tf_op jit(solution)/shard_map/sin | solution.py:102
  136.4 151.2 %all-to-all-done = f32[4,1,524288]{2,1,0:T(1,128)} async-done(((f32[4,1,524288]{2,1,0:T(1,128)}), f32[4,1,524288]{2,1,0:T(1,128)}, u32[]{:S(2)}, u32[]{:S(2)}) %all-to-all-start) | async-done | bytes 8388640 | tf_op jit(solution)/shard_map/all_to_all | solution.py:88
  288.2 28.5 %reduce.20 = f32[4,524288]{1,0:T(4,128)} reduce(f32[4,1,524288]{2,1,0:T(1,128)} %all-to-all-done, f32[]{:T(128)} %broadcast.1379), dimensions={1}, to_apply=%all_to_all.24.reduce_sub_computation | reduce | bytes 16777220 | tf_op jit(solution)/shard_map/all_to_all | solution.py:88
  316.8 16.8 %reshape.1131 = f32[1024,2,16,64]{3,2,1,0:T(8,128)} reshape(f32[4,524288]{1,0:T(4,128)} %reduce.20) | data formatting | bytes 16777216
  333.5 15.6 %copy.255 = f32[2,4,256,16,64]{2,3,1,0,4:T(8,128)} copy(f32[2,4,256,16,64]{4,3,0,2,1:T(8,128)} %bitcast.156) | data formatting | bytes 16777216 | tf_op jit(solution)/shard_map/all_to_all | solution.py:88
  349.1 21.3 %convolution_bitcast_fusion = f32[2,256,64,64]{1,2,3,0:T(8,128)S(1)} fusion(f32[2,256,64,64,1]{1,2,0,3,4:T(8,128)} %bitcast.157, f32[1,2,64,64]{2,3,0,1:T(8,128)S(1)} %get-tuple-element.94, f32[1,2,64,64]{2,3,0,1:T(8,128)S(1)} %get-tuple-element.97), kind=kOutput, calls=%fused_computation.105 | convolution fusion | flops 3221241856 | bytes 16842752 | tf_op jit(solution)/shard_map/prun,pquk->qrkn/dot_general | solution.py:86
  373.0 12.9 %fusion.41 = f32[2,256,64,64]{1,2,3,0:T(8,128)S(1)} fusion(f32[2,256,64,64]{1,2,3,0:T(8,128)S(1)} %pad_maximum_fusion.1, f32[1,2,64,64]{2,3,0,1:T(8,128)S(1)} %get-tuple-element.94, f32[1,2,64,64]{2,3,0,1:T(8,128)S(1)} %get-tuple-element.97), kind=kOutput, calls=%fused_computation.102 | convolution fusion | flops 3221241856 | bytes 16842752 | tf_op jit(solution)/shard_map/prkv,pqvj->qrjk/dot_general | solution.py:93
  408.8 32.3 %slice.243 = f32[2,1,4096]{1,2,0:T(8,128)} reverse(f32[2,1,4096]{1,2,0:T(8,128)} %get-tuple-element.84), dimensions={2} | reverse | bytes 65536 | tf_op jit(solution)/shard_map/slice | solution.py:54
  448.3 63.9 %rev.16 = f32[2,256,4096]{1,2,0:T(8,128)} reverse(f32[2,256,4096]{1,2,0:T(8,128)} %pad_maximum_fusion.2), dimensions={2} | reverse | bytes 16777216 | tf_op jit(solution)/shard_map/jit(_flip)/rev | solution.py:51
  516.9 11.2 scatter.14
  548.3 11.3 scatter.15
  559.6 23.3 %multiply_subtract_fusion.2 = (f32[1,256,4096]{1,2,0:T(8,128)}, f32[1,256,4096]{1,2,0:T(8,128)}, f32[1,256,4096]{1,2,0:T(8,128)}, f32[1,256,4096]{1,2,0:T(8,128)}) fusion(s32[4096]{0:T(1024)S(1)} %iota_multiply_fusion, s32[256]{0:T(256)S(1)} %dynamic_slice.3, f32[1,256,64,64]{1,3,2,0:T(8,128)} %copy.261, f32[1,256,64,64]{1,3,2,0:T(8,128)} %copy.262, ...), kind=kLoop, calls=%fused_computation.90 | loop fusion | flops 26214400 | bytes 33571840 | tf_op jit(solution)/shard_map/sub | solution.py:35
  582.9 9.3 fusion.5
  612.5 32.3 %slice.258 = f32[2,1,4096]{1,2,0:T(8,128)} reverse(f32[2,1,4096]{1,2,0:T(8,128)} %get-tuple-element.77), dimensions={2} | reverse | bytes 65536 | tf_op jit(solution)/shard_map/slice | solution.py:54
  652.0 63.9 %rev.18 = f32[2,256,4096]{1,2,0:T(8,128)} reverse(f32[2,256,4096]{1,2,0:T(8,128)} %pad_maximum_fusion.3), dimensions={2} | reverse | bytes 16777216 | tf_op jit(solution)/shard_map/jit(_flip)/rev | solution.py:51
  720.7 11.3 scatter.16
  740.8 11.2 scatter.19
  766.1 20.7 %slice_subtract_fusion = (f32[1,256,4096]{1,2,0:T(8,128)S(1)}, f32[1,256,4096]{1,2,0:T(8,128)S(1)}) fusion(f32[2,256,4096]{1,2,0:T(8,128)} %get-tuple-element.62, f32[2,256,4096]{1,2,0:T(8,128)S(1)} %get-tuple-element.61, s32[4096]{0:T(1024)S(1)} %iota_multiply_fusion, s32[256]{0:T(256)S(1)} %dynamic_slice.3), kind=kLoop, calls=%fused_computation.61 | loop fusion | flops 24117248 | bytes 25183232 | tf_op jit(solution)/shard_map/sub | solution.py:108
  791.8 8.9 fusion.47
  807.0 8.5 fusion.44
  822.0 18.0 %fusion.31 = (f32[1,256,4,1024]{1,3,2,0:T(8,128)S(1)}, f32[1,256,4,1024]{1,3,2,0:T(8,128)S(1)}) fusion(s32[4,1024]{1,0:T(4,128)S(1)} %copy-done.15, s32[256]{0:T(256)S(1)} %dynamic_slice.3, f32[1,256,4,1024]{1,3,2,0:T(8,128)S(1)} %bitcast.159, f32[1,256,4,1024]{1,3,2,0:T(8,128)S(1)} %bitcast.160), kind=kLoop, calls=%fused_computation.76 | loop fusion | flops 22020096 | bytes 16794624 | tf_op jit(solution)/shard_map/sub | solution.py:35
  850.0 11.8 maximum_bitcast_fusion
  861.8 170.4 %all-to-all-done.1 = f32[2,256,4,1024]{1,3,0,2:T(8,128)} async-done(((f32[2,256,4,1024]{1,3,0,2:T(8,128)}), f32[2,256,4,1024]{1,3,0,2:T(8,128)}, u32[]{:S(2)}, u32[]{:S(2)}) %all-to-all-start.1) | async-done | bytes 8388640 | tf_op jit(solution)/shard_map/all_to_all | solution.py:128
  1032.2 8.7 copy.277
  1040.9 62.8 %fusion.48 = f32[2,1024,1024]{2,1,0:T(8,128)S(1)} fusion(f32[2,1024,1024,1]{2,1,3,0:T(8,128)} %bitcast.167, f32[1,2,1024,1024]{2,3,1,0:T(8,128)} %get-tuple-element.88, f32[1,2,1024,1024]{2,3,1,0:T(8,128)} %get-tuple-element.87), kind=kOutput, calls=%fused_computation.106 | convolution fusion | flops 51543801856 | bytes 33554432 | tf_op jit(solution)/shard_map/pron,pqrm->qmon/dot_general | solution.py:126
  1108.6 23.0 %collective-permute-done = f32[2,256,1024]{2,1,0:T(8,128)S(1)} collective-permute-done((f32[2,256,1024]{2,1,0:T(8,128)S(1)}, f32[2,256,1024]{2,1,0:T(8,128)S(1)}, u32[]{:S(2)}, u32[]{:S(2)}) %collective-permute-start) | collective-permute-done | bytes 2097184 | tf_op jit(solution)/shard_map/ppermute | solution.py:17
  1136.3 23.0 %collective-permute-done.1 = f32[2,256,1024]{2,1,0:T(8,128)S(1)} collective-permute-done((f32[2,256,1024]{2,1,0:T(8,128)S(1)}, f32[2,256,1024]{2,1,0:T(8,128)S(1)}, u32[]{:S(2)}, u32[]{:S(2)}) %collective-permute-start.1) | collective-permute-done | bytes 2097184 | tf_op jit(solution)/shard_map/ppermute | solution.py:17
  1164.2 23.0 %collective-permute-done.2 = f32[2,256,1024]{2,1,0:T(8,128)S(1)} collective-permute-done((f32[2,256,1024]{2,1,0:T(8,128)S(1)}, f32[2,256,1024]{2,1,0:T(8,128)S(1)}, u32[]{:S(2)}, u32[]{:S(2)}) %collective-permute-start.2) | collective-permute-done | bytes 2097184 | tf_op jit(solution)/shard_map/ppermute | solution.py:17
  (103 shorter events, 199.3 us)
Async XLA Ops:
  0.0 4.6 copy-start
  98.2 189.5 %all-to-all-start = ((f32[4,1,524288]{2,1,0:T(1,128)}), f32[4,1,524288]{2,1,0:T(1,128)}, u32[]{:S(2)}, u32[]{:S(2)}) async-start(f32[4,1,524288]{2,1,0:T(1,128)} %reshape.1130), calls=%async_computation | async-start | bytes 16777216 | tf_op jit(solution)/shard_map/all_to_all | solution.py:88
  133.9 236.5 %copy-start.12 = (f32[64,64]{0,1:T(8,128)}, f32[64,64]{0,1:T(8,128)S(1)}, u32[]{:S(2)}) copy-start(f32[64,64]{0,1:T(8,128)S(1)} %get-tuple-element.112) | copy-start | bytes 49156
  390.8 4.7 copy-start.2
  537.2 6.7 copy-start.9
  582.9 9.4 copy-start.7
  582.9 10.7 copy-start.8
  594.7 2.0 copy-start.3
  594.8 3.3 copy-start.5
  752.0 7.7 copy-start.4
  752.0 7.7 copy-start.6
  789.3 2.5 copy-start.10
  789.3 2.5 copy-start.11
  800.7 4.9 copy-start.13
  800.7 4.9 copy-start.14
  819.1 2.9 copy-start.15
  844.3 187.9 %all-to-all-start.1 = ((f32[2,256,4,1024]{1,3,0,2:T(8,128)}), f32[2,256,4,1024]{1,3,0,2:T(8,128)}, u32[]{:S(2)}, u32[]{:S(2)}) async-start(f32[2,256,4,1024]{1,3,0,2:T(8,128)} %copy.276), calls=%async_computation.1 | async-start | bytes 16777216 | tf_op jit(solution)/shard_map/all_to_all | solution.py:128
  1104.0 27.5 %collective-permute-start = (f32[2,256,1024]{2,1,0:T(8,128)S(1)}, f32[2,256,1024]{2,1,0:T(8,128)S(1)}, u32[]{:S(2)}, u32[]{:S(2)}) collective-permute-start(f32[2,256,1024]{2,1,0:T(8,128)S(1)} %slice.311), channel_id=1, source_target_pairs={{0,4},{4,8},{8,12},{12,16},{16,20},{20,24},{24,28},{1,5},{5,9},{9,... | collective-permute-start | bytes 6291464 | tf_op jit(solution)/shard_map/ppermute | solution.py:17
  1131.9 27.4 %collective-permute-start.1 = (f32[2,256,1024]{2,1,0:T(8,128)S(1)}, f32[2,256,1024]{2,1,0:T(8,128)S(1)}, u32[]{:S(2)}, u32[]{:S(2)}) collective-permute-start(f32[2,256,1024]{2,1,0:T(8,128)S(1)} %slice_add_fusion.1), channel_id=1, source_target_pairs={{0,4},{4,8},{8,12},{12,16},{16,20},{20,24},{24,28},{1,5},{5,9},{9,... | collective-permute-start | bytes 6291464 | tf_op jit(solution)/shard_map/ppermute | solution.py:17
  1159.3 29.6 %copy-start.1 = (f32[1,2,256,1024]{3,2,1,0:T(8,128)S(1)}, f32[1,2,256,1024]{3,2,1,0:T(8,128)}, u32[]{:S(2)}) copy-start(f32[1,2,256,1024]{3,2,1,0:T(8,128)} %param.10) | copy-start | bytes 6291460
  1159.7 27.5 %collective-permute-start.2 = (f32[2,256,1024]{2,1,0:T(8,128)S(1)}, f32[2,256,1024]{2,1,0:T(8,128)S(1)}, u32[]{:S(2)}, u32[]{:S(2)}) collective-permute-start(f32[2,256,1024]{2,1,0:T(8,128)S(1)} %slice_add_fusion.2), channel_id=1, source_target_pairs={{0,4},{4,8},{8,12},{12,16},{16,20},{20,24},{24,28},{1,5},{5,9},{9,... | collective-permute-start | bytes 6291464 | tf_op jit(solution)/shard_map/ppermute | solution.py:17
where the time goes:
time: 1210 us; the launch traced here: 1190 us
  local copies, waits for them, and re-layouts  428 us (35%)
  waiting for transfers between devices  390 us (32%)
  other arithmetic  216 us (18%)
  matrix products  129 us (11%)
  starting transfers between devices  24.9 us (2%)
    all_to_all x1, waiting for transfers between devices, per_device(): lax.all_to_all(packed, 'fft', split_axis=2, concat_axis=1, tiled=True)  170 us
    all_to_all x1, waiting for transfers between devices, per_device(): lax.all_to_all(spread, 'fft', split_axis=1, concat_axis=2, tiled=True)  151 us
    rev x2, local copies, waits for them, and re-layouts, mirrored(): flipped = jnp.flip(swapped, axis=2)  128 us
    slice x4, local copies, waits for them, and re-layouts, mirrored(): flipped = flipped.at[:, 0].set(jnp.where(is_first, zero_row, flipped[:, 0]))  73.2 us
    ppermute x3, waiting for transfers between devices, passed_along(): return lax.ppermute(shard, axis, pairs)  68.9 us
    dot_general x1, matrix products, per_device(): jnp.einsum('pron,pqrm->qmon', lax.all_to_all(packed, 'fft', split_axis=2,...  62.8 us
    sub x5, other arithmetic, complex_mul(): first = left_pair[0] * right_pair[0] - left_pair[1] * right_pair[1]  45.3 us
    unnamed x36, local copies, waits for them, and re-layouts  41.4 us
  transfers between devices with their start and end apart: 5, of which 5 were waited for; matrix products, arithmetic and copies ran while one was open for 4% of the time, Pallas kernels for 0%

commit v1 on v0

v1 whole, which is shorter than its diff:
```python
import functools
import math

import jax
import jax.numpy as jnp
import ml_dtypes
import numpy as np
from jax import lax
from jax.experimental import pallas as pl
from jax.experimental.pallas import tpu as pltpu
from jax.sharding import PartitionSpec as P

LANES = 128
SUB = 8
VMEM = 50 * 1024 * 1024


def passed_along(shard, axis, by):
    length = lax.axis_size(axis)
    pairs = [(i, i + by) for i in range(length) if 0 <= i + by < length]
    return lax.ppermute(shard, axis, pairs)


def turn(products, period):
    angles = np.mod(products, period).astype(np.float64) * (-2.0 * math.pi / period)
    return np.cos(angles), np.sin(angles)


def halves(table):
    high = table.astype(ml_dtypes.bfloat16)
    low = (table - high.astype(np.float64)).astype(ml_dtypes.bfloat16)
    return high, low


def split(values):
    high = values.astype(jnp.bfloat16)
    low = (values - high.astype(jnp.float32)).astype(jnp.bfloat16)
    return high, low


def dot(left, right):
    return jnp.dot(left, right, preferred_element_type=jnp.float32)


def dot3(left_high, left_low, right_high, right_low):
    return dot(left_high, right_high) + (dot(left_high, right_low) + dot(left_low, right_high))


def scale_by(value, cos, sin):
    re, im = value
    near = 1e-12
    if abs(sin) < near:
        return value if cos > 0 else (-re, -im)
    if abs(cos) < near:
        return (-im, re) if sin > 0 else (im, -re)
    if abs(abs(cos) - abs(sin)) < near:
        size = abs(cos)
        first = re if cos > 0 else -re
        second = im if cos > 0 else -im
        third = im if sin > 0 else -im
        fourth = re if sin > 0 else -re
        return (first - third) * size, (second + fourth) * size
    return re * cos - im * sin, re * sin + im * cos


def plus(left, right):
    return left[0] + right[0], left[1] + right[1]


def minus(left, right):
    return left[0] - right[0], left[1] - right[1]


def small_dft(values, sign):
    count = len(values)
    if count == 1:
        return values
    if count == 2:
        return [plus(values[0], values[1]), minus(values[0], values[1])]
    if count == 4:
        even_sum, even_gap = plus(values[0], values[2]), minus(values[0], values[2])
        odd_sum, odd_gap = plus(values[1], values[3]), minus(values[1], values[3])
        turned = scale_by(odd_gap, 0.0, float(sign))
        return [plus(even_sum, odd_sum), plus(even_gap, turned), minus(even_sum, odd_sum), minus(even_gap, turned)]
    radix = 4 if count == 32 else 2
    part = count // radix
    pieces = [small_dft(values[i::radix], sign) for i in range(radix)]
    result = [None] * count
    for k in range(part):
        column = []
        for i in range(radix):
            angle = sign * 2.0 * math.pi * i * k / count
            column.append(scale_by(pieces[i][k], math.cos(angle), math.sin(angle)))
        for q, value in enumerate(small_dft(column, sign)):
            result[k + part * q] = value
    return result


def spread_kernel(x0, x3, x2, x1, table_high, table_low, turns, phases, out, high, low):
    quarter, width = x0.shape[2], x0.shape[3]

    @pl.when(pl.program_id(0) == 0)
    def _():
        for block, ref in enumerate((x0, x3, x2, x1)):
            for parity in range(2):
                first, second = split(ref[0, parity])
                rows = pl.ds(block * quarter, quarter)
                high[rows, pl.ds(parity * width, width)] = first
                low[rows, pl.ds(parity * width, width)] = second

    sums = dot3(table_high[0], table_low[0], high[...], low[...])
    slots = sums.shape[0] // 2
    turn_re, turn_im = turns[0, 0], turns[0, 1]
    for parity in range(2):
        ph_re, ph_im = phases[0, 2 * parity], phases[0, 2 * parity + 1]
        re = sums[:slots, parity * width : (parity + 1) * width]
        im = sums[slots:, parity * width : (parity + 1) * width]
        w_re = turn_re * ph_re - turn_im * ph_im
        w_im = turn_re * ph_im + turn_im * ph_re
        out[0, parity, 0] = re * w_re - im * w_im
        out[0, parity, 1] = re * w_im + im * w_re


def middle_kernel(chunks, with_extra, device, *refs):
    pieces = refs[:chunks]
    chirp, twist, tab_high, tab_low, extra_turn, out = refs[chunks : chunks + 6]
    data, grid_a, kept = refs[chunks + 6 :]
    groups = pieces[0].shape[0]
    tiles = pieces[0].shape[4] // LANES
    per_group = tiles * chunks
    points = groups * per_group
    step = pl.program_id(0)
    is_first = device[0] == 0
    if with_extra:
        on_extra = jnp.logical_and(is_first, step == 0)
        on_zero = jnp.logical_and(is_first, step == 1)
        active = jnp.logical_or(is_first, step > 0)
    rows = points * SUB

    def place(j):
        group, rest = divmod(j, per_group)
        chunk, tile = divmod(rest, tiles)
        return pieces[chunk], group, pl.ds(tile * LANES, LANES)

    def outlet(j):
        group, tile = divmod(j, per_group)
        return group, pl.ds(tile * LANES, LANES)

    def load_plain():
        for j in range(points):
            ref, group, lanes = place(j)
            for parity in range(2):
                for part in range(2):
                    data[parity, part, j] = ref[group, parity, part, :, lanes]

    def load_extra():
        for j in range(points):
            ref, group, lanes = place(j)
            for parity in range(2):
                value = ref[group, parity, 1, :, lanes]
                for part in range(2):
                    data[parity, part, j] = value * extra_turn[parity, part, pl.ds(j, 1)]

    def run():
        spectra = []
        for parity in range(2):
            values = [(data[parity, 0, j], data[parity, 1, j]) for j in range(points)]
            for k, (re, im) in enumerate(small_dft(values, -1)):
                w_re, w_im = twist[parity, 0, pl.ds(k, 1)], twist[parity, 1, pl.ds(k, 1)]
                grid_a[pl.ds(k * SUB, SUB), pl.ds(0, LANES)] = re * w_re - im * w_im
                grid_a[pl.ds(k * SUB, SUB), pl.ds(LANES, LANES)] = re * w_im + im * w_re
            high, low = split(grid_a[...])
            spectra.append(dot3(high, low, tab_high[parity], tab_low[parity]))
        even, odd = spectra
        upper, lower = even + odd, even - odd
        u_re, u_im = upper[:, :LANES], upper[:, LANES:]
        l_re, l_im = lower[:, :LANES], lower[:, LANES:]
        c1r, c1i, c2r, c2i = (chirp[0, n].reshape(rows, LANES) for n in range(4))
        f_re, f_im = u_re * c1r - u_im * c1i, u_re * c1i + u_im * c1r
        g_re, g_im = l_re * c2r + l_im * c2i, l_im * c2r - l_re * c2i
        sides = ((f_re + g_re, f_im + g_im), (f_re - g_re, f_im - g_im))
        for parity in range(2):
            high, low = split(jnp.concatenate(sides[parity], axis=1))
            grid_a[...] = dot3(high, low, tab_high[2 + parity], tab_low[2 + parity])
            values = []
            for k in range(points):
                re = grid_a[pl.ds(k * SUB, SUB), pl.ds(0, LANES)]
                im = grid_a[pl.ds(k * SUB, SUB), pl.ds(LANES, LANES)]
                w_re, w_im = twist[parity, 0, pl.ds(k, 1)], twist[parity, 1, pl.ds(k, 1)]
                values.append((re * w_re + im * w_im, im * w_re - re * w_im))
            for j, (re, im) in enumerate(small_dft(values, 1)):
                group, lanes = outlet(j)
                out[group, parity, 0, :, lanes] = re
                out[group, parity, 1, :, lanes] = im

    if not with_extra:
        load_plain()
        run()
        return

    @pl.when(on_extra)
    def _():
        load_extra()

    @pl.when(step > 0)
    def _():
        load_plain()

    keep = lax.broadcasted_iota(jnp.int32, (SUB, LANES), 0) > 0

    @pl.when(on_zero)
    def _():
        for parity in range(2):
            for j in range(points):
                data[parity, 1, j] = jnp.where(keep, data[parity, 1, j], 0.0)

    @pl.when(active)
    def _():
        run()

    @pl.when(on_extra)
    def _():
        for parity in range(2):
            for j in range(points):
                group, lanes = outlet(j)
                w_re, w_im = extra_turn[parity, 0, pl.ds(j, 1)], extra_turn[parity, 1, pl.ds(j, 1)]
                kept[parity, j] = out[group, parity, 0, :, lanes] * w_re + out[group, parity, 1, :, lanes] * w_im

    @pl.when(on_zero)
    def _():
        for parity in range(2):
            for j in range(points):
                group, lanes = outlet(j)
                out[group, parity, 1, :, lanes] = jnp.where(keep, out[group, parity, 1, :, lanes], kept[parity, j])


def gather_kernel(chunks, *refs):
    pieces = refs[:chunks]
    turns, phases, table_high, table_low, out, high, low = refs[chunks:]
    groups, slots, width = pieces[0].shape[0], pieces[0].shape[3], pieces[0].shape[4]
    row = 0
    for chunk, ref in enumerate(pieces):
        own = pl.ds(chunk * slots, slots)
        for group in range(groups):
            t_re, t_im = turns[group, 0, own], turns[group, 1, own]
            for parity in range(2):
                ph_re, ph_im = phases[group, 2 * parity, own], phases[group, 2 * parity + 1, own]
                w_re = t_re * ph_re - t_im * ph_im
                w_im = t_re * ph_im + t_im * ph_re
                re, im = ref[group, parity, 0], ref[group, parity, 1]
                lanes = pl.ds(parity * width, width)
                for part, value in enumerate((re * w_re + im * w_im, im * w_re - re * w_im)):
                    first, second = split(value)
                    high[pl.ds(row + part * slots, slots), lanes] = first
                    low[pl.ds(row + part * slots, slots), lanes] = second
            row += 2 * slots
    sums = dot3(table_high[...], table_low[...], high[...], low[...])
    for parity in range(2):
        out[0, parity] = sums[:, parity * width : (parity + 1) * width]


def whole(shape):
    return pl.BlockSpec(shape, lambda i: (0,) * len(shape))


def params():
    return pltpu.CompilerParams(vmem_limit_bytes=VMEM, dimension_semantics=("arbitrary",))


def estimate(flops, size):
    return pl.CostEstimate(flops=int(flops), bytes_accessed=int(size), transcendentals=0)


def per_device(col_chunks, row_chunks, voltage, chirp_phase):
    groups = lax.axis_size("fft")
    device = lax.axis_index("fft")
    quarter, width = voltage.shape[2], voltage.shape[3]
    row_count = 4 * quarter
    half = row_count // 2
    columns = width * groups
    slots = half // groups
    total = row_count * columns
    first_len = columns // LANES
    col_width = width // col_chunks
    row_slots = slots // row_chunks
    blocks = slots // SUB
    step_blocks = blocks // row_chunks

    rows = np.arange(half)
    times = np.arange(row_count)
    cos, sin = turn(rows[:, None] * times[None, :], row_count)
    sin[0] = np.where(times % 2 == 0, 1.0, -1.0)
    spread_table = np.stack([cos, sin]).reshape(2, groups, slots, row_count)
    spread_high, spread_low = halves(spread_table.transpose(1, 0, 2, 3).reshape(groups, 2 * slots, row_count))

    cos, sin = turn(rows[:, None] * np.arange(width)[None, :], total)
    turns = np.stack([cos, sin]).reshape(2, groups, slots, width).transpose(1, 0, 2, 3).astype(np.float32)

    zs = np.arange(groups)[:, None]
    even_phase = np.stack(turn(rows[None, :] * (zs * width), total), axis=1)
    odd_phase = np.stack(turn(rows[None, :] * (2 * zs * width + 1), 2 * total), axis=1)
    phase_table = np.concatenate([even_phase, odd_phase], axis=1).reshape(groups, 4, groups, slots)
    phase_table = phase_table.transpose(0, 2, 1, 3)[..., None].astype(np.float32)
    phases = lax.dynamic_index_in_dim(jnp.asarray(phase_table), device, 0, keepdims=False)

    keys = np.arange(first_len)
    lanes = np.arange(LANES)
    twist = np.stack(
        [
            np.stack(turn(keys[:, None] * lanes[None, :], columns)),
            np.stack(turn(keys[:, None] * (2 * lanes[None, :] + 1), 2 * columns)),
        ]
    ).astype(np.float32)
    tables = []
    for cos, sin in (
        turn(lanes[:, None] * lanes[None, :], LANES),
        turn((2 * lanes[:, None] + 1) * lanes[None, :], 2 * LANES),
    ):
        tables.append(np.block([[cos, sin], [-sin, cos]]))
    tables = np.stack(tables + [table.T for table in tables])
    tab_high, tab_low = halves(tables)
    every = (LANES * keys[:, None] + lanes[None, :])
    extra_turn = np.stack(
        [np.stack(turn(half * every, total)), np.stack(turn(half * (2 * every + 1), 2 * total))]
    ).astype(np.float32)

    cos, sin = turn(rows[None, :] * np.arange(quarter)[:, None], row_count)
    cos[:, 0] = 0.5
    sin[:, 0] = np.where(np.arange(quarter) % 2 == 0, 0.5, -0.5)
    gather_table = np.stack([cos, sin], axis=1) / total
    gather_table = gather_table.reshape(quarter, 2, groups, row_chunks, row_slots)
    gather_table = gather_table.transpose(0, 3, 2, 1, 4).reshape(quarter, 2 * half)
    gather_high, gather_low = halves(gather_table)

    spread_call = [
        pl.pallas_call(
            spread_kernel,
            grid=(groups,),
            in_specs=[pl.BlockSpec((1, 2, quarter, col_width), lambda d: (0, 0, 0, 0))] * 4
            + [pl.BlockSpec((1, 2 * slots, row_count), lambda d: (d, 0, 0))] * 2
            + [
                pl.BlockSpec((1, 2, slots, col_width), lambda d, c=chunk: (d, 0, 0, c)),
                pl.BlockSpec((1, 4, slots, 1), lambda d: (d, 0, 0, 0)),
            ],
            out_specs=pl.BlockSpec((1, 2, 2, slots, col_width), lambda d: (d, 0, 0, 0, 0)),
            out_shape=jax.ShapeDtypeStruct((groups, 2, 2, slots, col_width), jnp.float32),
            scratch_shapes=[pltpu.VMEM((row_count, 2 * col_width), jnp.bfloat16)] * 2,
            compiler_params=params(),
            cost_estimate=estimate(12 * row_count * row_count * col_width, 16 * row_count * col_width),
            name="spread",
        )
        for chunk in range(col_chunks)
    ]

    received = []
    for chunk in range(col_chunks):
        own = voltage[..., chunk * col_width : (chunk + 1) * col_width]
        one = passed_along(own, "seg", 1)
        two = passed_along(one, "seg", 1)
        three = passed_along(two, "seg", 1)
        sent = spread_call[chunk](own, three, two, one, spread_high, spread_low, turns, phases)
        received.append(lax.all_to_all(sent, "fft", split_axis=0, concat_axis=0, tiled=True))

    is_first = device == 0
    digits = chirp_phase.reshape(2, slots, LANES, first_len)
    near, far = digits[0], digits[1, :, ::-1, ::-1]
    zero_row = jnp.roll(jnp.flip(chirp_phase[0, 0]), 1).reshape(LANES, first_len)
    at_zero = jnp.logical_and(is_first, jnp.arange(slots) == 0)[:, None, None]
    extra = jnp.pad(jnp.stack([digits[1, 0], far[0]])[:, None], ((0, 0), (0, SUB - 1), (0, 0), (0, 0)))
    far = jnp.where(at_zero, zero_row[None], far)
    angles = jnp.concatenate([extra, jnp.stack([near, far])], axis=1)
    angles = angles.reshape(2, blocks + 1, SUB, LANES, first_len).transpose(1, 0, 4, 2, 3)
    dead = (
        (lax.broadcasted_iota(jnp.int32, angles.shape, 0) == 1)
        & (lax.broadcasted_iota(jnp.int32, angles.shape, 2) == 0)
        & (lax.broadcasted_iota(jnp.int32, angles.shape, 3) == 0)
        & (lax.broadcasted_iota(jnp.int32, angles.shape, 4) == 0)
        & is_first
    )
    chirp = jnp.stack([jnp.where(dead, 0.0, jnp.cos(angles)), jnp.where(dead, 0.0, jnp.sin(angles))], axis=2)
    chirp = chirp.reshape(blocks + 1, 4, first_len, SUB, LANES)

    device_word = device.astype(jnp.int32).reshape(1)
    returned = []
    for chunk in range(row_chunks):
        with_extra = chunk == 0
        base = chunk * step_blocks
        lag = 1 if with_extra else 0

        def inlet(i, base=base, lag=lag):
            return (0, 0, 0, base + jnp.maximum(i - lag, 0), 0)

        def outlet(i, lag=lag):
            return (0, 0, 0, jnp.maximum(i - lag, 0), 0)

        def chirp_at(i, base=base, lag=lag):
            return (base + 1 - lag + i, 0, 0, 0, 0)

        sent = pl.pallas_call(
            functools.partial(middle_kernel, col_chunks, with_extra),
            grid=(step_blocks + lag,),
            in_specs=[pl.BlockSpec(memory_space=pltpu.SMEM)]
            + [pl.BlockSpec((groups, 2, 2, SUB, col_width), inlet)] * col_chunks
            + [
                pl.BlockSpec((1, 4, first_len, SUB, LANES), chirp_at),
                whole(twist.shape),
                whole(tab_high.shape),
                whole(tab_low.shape),
                whole(extra_turn.shape),
            ],
            out_specs=pl.BlockSpec((groups, 2, 2, SUB, width), outlet),
            out_shape=jax.ShapeDtypeStruct((groups, 2, 2, row_slots, width), jnp.float32),
            scratch_shapes=[
                pltpu.VMEM((2, 2, first_len, SUB, LANES), jnp.float32),
                pltpu.VMEM((first_len * SUB, 2 * LANES), jnp.float32),
                pltpu.VMEM((2, first_len, SUB, LANES), jnp.float32),
            ],
            compiler_params=params(),
            cost_estimate=estimate(2e9 / row_chunks, 25e6 / row_chunks),
            name="middle",
        )(device_word, *received, chirp, twist, tab_high, tab_low, extra_turn)
        returned.append(lax.all_to_all(sent, "fft", split_axis=0, concat_axis=0, tiled=True))

    tile = min(width, 2 * LANES)
    return pl.pallas_call(
        functools.partial(gather_kernel, row_chunks),
        grid=(width // tile,),
        in_specs=[pl.BlockSpec((groups, 2, 2, row_slots, tile), lambda c: (0, 0, 0, 0, c))] * row_chunks
        + [
            pl.BlockSpec((groups, 2, slots, tile), lambda c: (0, 0, 0, c)),
            whole((groups, 4, slots, 1)),
            whole(gather_high.shape),
            whole(gather_low.shape),
        ],
        out_specs=pl.BlockSpec((1, 2, quarter, tile), lambda c: (0, 0, 0, c)),
        out_shape=jax.ShapeDtypeStruct((1, 2, quarter, width), jnp.float32),
        scratch_shapes=[pltpu.VMEM((2 * half, 2 * tile), jnp.bfloat16)] * 2,
        compiler_params=params(),
        cost_estimate=estimate(12 * quarter * row_count * width, 20e6),
        name="gather",
    )(*returned, turns, phases, gather_high, gather_low)


def solution(mesh):
    in_specs = (P("seg", None, None, "fft"), P(None, "fft", None))
    out_specs = P("seg", None, None, "fft")
    return jax.shard_map(
        functools.partial(per_device, 4, 4),
        mesh=mesh,
        in_specs=in_specs,
        out_specs=out_specs,
        check_vma=False,
    )
```

time: 1210 us -> 484 us (0.40); the launches traced: 1190 us -> 475 us
  local copies, waits for them, and re-layouts: 428 us -> 45.7 us
  waiting for transfers between devices: 390 us -> 194 us
  other arithmetic: 216 us -> 22.5 us
  matrix products: 129 us -> 0 us
  starting transfers between devices: 24.9 us -> 98.3 us
  Pallas kernels: 0 us -> 63 us
  blocking collectives: 0 us -> 51.7 us
    all_to_all x2 -> x7, waiting for transfers between devices: 322 us -> 128 us  [per_device(): lax.all_to_all(sent, 'fft', split_axis=0, concat_axis=0, tiled=True)]
    rev x4 -> x1, local copies, waits for them, and re-layouts: 133 us -> 2.42 us  [per_device(): near, far = (digits[0], digits[1, :, ::-1, ::-1])]
    dot_general x6 -> x0, matrix products: 129 us -> none  [the longest x1 62.8 us: per_device(): jnp.einsum('pron,pqrm->qmon', lax.all_to_all(packed, 'fft', split_axis=2,...]
    slice x19 -> x10, local copies, waits for them, and re-layouts: 109 us -> 17 us  [the longest x3 9.89 us: per_device(): near, far = (digits[0], digits[1, :, ::-1, ::-1])]
    sub x6 -> x0, other arithmetic: 66 us -> none  [the longest x5 45.3 us: complex_mul(): first = left_pair[0] * right_pair[0] - left_pair[1] * right_pair[1]]
    pallas_call x0 -> x9, Pallas kernels: none -> 63 us  [the longest x4 28.6 us: per_device(): spread_call[chunk]]
    ppermute x3 -> x12, starting transfers between devices: 13.5 us -> 66.8 us  [passed_along(): return lax.ppermute(shard, axis, pairs)]
    all_to_all x0 -> x1, blocking collectives: none -> 51.7 us  [per_device(): lax.all_to_all(sent, 'fft', split_axis=0, concat_axis=0, tiled=True)]
  transfers between devices with their start and end apart: 5 -> 19, of which waited for: 5 -> 17; matrix products, arithmetic and copies ran while one was open for 4% -> 12% of each run, Pallas kernels for 0% -> 8%
where the time goes in v1:
time: 484 us; the launch traced here: 475 us
  waiting for transfers between devices  194 us (40%)
  starting transfers between devices  98.3 us (20%)
  Pallas kernels  63 us (13%)
  blocking collectives  51.7 us (11%)
  local copies, waits for them, and re-layouts  45.7 us (9%)
  other arithmetic  22.5 us (5%)
    all_to_all x7, waiting for transfers between devices, per_device(): lax.all_to_all(sent, 'fft', split_axis=0, concat_axis=0, tiled=True)  128 us
    ppermute x12, starting transfers between devices, passed_along(): return lax.ppermute(shard, axis, pairs)  66.8 us
    ppermute x12, waiting for transfers between devices, passed_along(): return lax.ppermute(shard, axis, pairs)  65.6 us
    all_to_all x1, blocking collectives, per_device(): lax.all_to_all(sent, 'fft', split_axis=0, concat_axis=0, tiled=True)  51.7 us
    all_to_all x7, starting transfers between devices, per_device(): lax.all_to_all(sent, 'fft', split_axis=0, concat_axis=0, tiled=True)  31.5 us
    pallas_call x4, Pallas kernels, per_device(): spread_call[chunk]  28.6 us
    pallas_call x4, Pallas kernels, per_device(): pl.pallas_call(functools.partial(middle_kernel, col_chunks, with_extra),...  25.4 us
    cos x1, other arithmetic, per_device(): jnp.cos(angles)  16.1 us
  transfers between devices with their start and end apart: 19, of which 17 were waited for; matrix products, arithmetic and copies ran while one was open for 12% of the time, Pallas kernels for 8%

profile of v1, /device:TPU:1, one launch (start us, length us, event | category | flops | bytes accessed | tf_op | source)
XLA Modules:
  0.0 475.3 jit_solution(4664562321681116667)
XLA Ops:
  6.3 6.1 %collective-permute-done.9.x1 = f32[1,2,256,256]{3,2,1,0:T(8,128)S(1)} collective-permute-done((f32[1,2,256,256]{3,2,1,0:T(8,128)S(1)}, f32[1,2,256,256]{3,2,1,0:T(8,128)S(1)}, u32[]{:S(2)}, u32[]{:S(2)}) %collective-permute-start.9) | collective-permute-done | bytes 524320 | tf_op jit(solution)/shard_map/ppermute | solution.py:21
  17.6 5.3 %collective-permute-done.10.x2 = f32[1,2,256,256]{3,2,1,0:T(8,128)} collective-permute-done((f32[1,2,256,256]{3,2,1,0:T(8,128)S(1)}, f32[1,2,256,256]{3,2,1,0:T(8,128)}, u32[]{:S(2)}, u32[]{:S(2)}) %collective-permute-start.10) | collective-permute-done | bytes 524320 | tf_op jit(solution)/shard_map/ppermute | solution.py:21
  28.4 5.3 %collective-permute-done.11.x3 = f32[1,2,256,256]{3,2,1,0:T(8,128)} collective-permute-done((f32[1,2,256,256]{3,2,1,0:T(8,128)}, f32[1,2,256,256]{3,2,1,0:T(8,128)}, u32[]{:S(2)}, u32[]{:S(2)}) %collective-permute-start.11) | collective-permute-done | bytes 524320 | tf_op jit(solution)/shard_map/ppermute | solution.py:21
  34.8 7.5 %spread.7 = f32[4,2,2,128,256]{4,3,2,1,0:T(8,128)} custom-call(f32[1,2,256,256]{3,2,1,0:T(8,128)S(1)} %get-tuple-element.9.x0, f32[1,2,256,256]{3,2,1,0:T(8,128)} %collective-permute-done.11.x3, f32[1,2,256,256]{3,2,1,0:T(8,128)} %collective-permute-done.10.x2, f32[1,2,256,256]{3,2,1,0:T(8,128)S(1)} %copy-done.11, ...), custom_call_target="tpu_custom_call" | custom-call | flops 3221225472 | bytes 4194304 | tf_op jit(solution)/shard_map/spread/pallas_call | solution.py:361
  42.4 4.6 all-to-all-start.3
  46.9 4.7 collective-permute-start.6
  51.6 6.1 %collective-permute-done.6.x1 = f32[1,2,256,256]{3,2,1,0:T(8,128)S(1)} collective-permute-done((f32[1,2,256,256]{3,2,1,0:T(8,128)S(1)}, f32[1,2,256,256]{3,2,1,0:T(8,128)S(1)}, u32[]{:S(2)}, u32[]{:S(2)}) %collective-permute-start.6) | collective-permute-done | bytes 524320 | tf_op jit(solution)/shard_map/ppermute | solution.py:21
  62.1 6.1 %collective-permute-done.7.x2 = f32[1,2,256,256]{3,2,1,0:T(8,128)S(1)} collective-permute-done((f32[1,2,256,256]{3,2,1,0:T(8,128)S(1)}, f32[1,2,256,256]{3,2,1,0:T(8,128)S(1)}, u32[]{:S(2)}, u32[]{:S(2)}) %collective-permute-start.7) | collective-permute-done | bytes 524320 | tf_op jit(solution)/shard_map/ppermute | solution.py:21
  72.6 6.1 %collective-permute-done.8.x3 = f32[1,2,256,256]{3,2,1,0:T(8,128)S(1)} collective-permute-done((f32[1,2,256,256]{3,2,1,0:T(8,128)S(1)}, f32[1,2,256,256]{3,2,1,0:T(8,128)S(1)}, u32[]{:S(2)}, u32[]{:S(2)}) %collective-permute-start.8) | collective-permute-done | bytes 524320 | tf_op jit(solution)/shard_map/ppermute | solution.py:21
  78.7 7.0 %spread.6 = f32[4,2,2,128,256]{4,3,2,1,0:T(8,128)} custom-call(f32[1,2,256,256]{3,2,1,0:T(8,128)S(1)} %get-tuple-element.12.x0, f32[1,2,256,256]{3,2,1,0:T(8,128)S(1)} %collective-permute-done.8.x3, f32[1,2,256,256]{3,2,1,0:T(8,128)S(1)} %collective-permute-done.7.x2, f32[1,2,256,256]{3,2,1,0:T(8,128)S(1)} %collective-permute-done.6.x1, ...), custom_call_target="tpu_custom_call" | custom-call | flops 3221225472 | bytes 4194304 | tf_op jit(solution)/shard_map/spread/pallas_call | solution.py:361
  94.1 11.4 %collective-permute-start.3 = (f32[1,2,256,256]{3,2,1,0:T(8,128)S(1)}, f32[1,2,256,256]{3,2,1,0:T(8,128)S(1)}, u32[]{:S(2)}, u32[]{:S(2)}) collective-permute-start(f32[1,2,256,256]{3,2,1,0:T(8,128)S(1)} %get-tuple-element.10.x0), channel_id=1, source_target_pairs={{0,4},{4,8},{8,12},{12,16},{16,20},{20,24},{24,28},{1,5},{5,9},{9,... | collective-permute-start | bytes 1572872 | tf_op jit(solution)/shard_map/ppermute | solution.py:21
  105.5 6.1 %collective-permute-done.3.x1 = f32[1,2,256,256]{3,2,1,0:T(8,128)S(1)} collective-permute-done((f32[1,2,256,256]{3,2,1,0:T(8,128)S(1)}, f32[1,2,256,256]{3,2,1,0:T(8,128)S(1)}, u32[]{:S(2)}, u32[]{:S(2)}) %collective-permute-start.3) | collective-permute-done | bytes 524320 | tf_op jit(solution)/shard_map/ppermute | solution.py:21
  116.0 6.1 %collective-permute-done.4.x2 = f32[1,2,256,256]{3,2,1,0:T(8,128)S(1)} collective-permute-done((f32[1,2,256,256]{3,2,1,0:T(8,128)S(1)}, f32[1,2,256,256]{3,2,1,0:T(8,128)S(1)}, u32[]{:S(2)}, u32[]{:S(2)}) %collective-permute-start.4) | collective-permute-done | bytes 524320 | tf_op jit(solution)/shard_map/ppermute | solution.py:21
  126.4 6.1 %collective-permute-done.5.x3 = f32[1,2,256,256]{3,2,1,0:T(8,128)S(1)} collective-permute-done((f32[1,2,256,256]{3,2,1,0:T(8,128)S(1)}, f32[1,2,256,256]{3,2,1,0:T(8,128)S(1)}, u32[]{:S(2)}, u32[]{:S(2)}) %collective-permute-start.5) | collective-permute-done | bytes 524320 | tf_op jit(solution)/shard_map/ppermute | solution.py:21
  132.5 7.1 %spread.5 = f32[4,2,2,128,256]{4,3,2,1,0:T(8,128)} custom-call(f32[1,2,256,256]{3,2,1,0:T(8,128)S(1)} %get-tuple-element.10.x0, f32[1,2,256,256]{3,2,1,0:T(8,128)S(1)} %collective-permute-done.5.x3, f32[1,2,256,256]{3,2,1,0:T(8,128)S(1)} %collective-permute-done.4.x2, f32[1,2,256,256]{3,2,1,0:T(8,128)S(1)} %collective-permute-done.3.x1, ...), custom_call_target="tpu_custom_call" | custom-call | flops 3221225472 | bytes 4194304 | tf_op jit(solution)/shard_map/spread/pallas_call | solution.py:361
  147.3 11.1 %collective-permute-start = (f32[1,2,256,256]{3,2,1,0:T(8,128)S(1)}, f32[1,2,256,256]{3,2,1,0:T(8,128)S(1)}, u32[]{:S(2)}, u32[]{:S(2)}) collective-permute-start(f32[1,2,256,256]{3,2,1,0:T(8,128)S(1)} %get-tuple-element.11.x0), channel_id=1, source_target_pairs={{0,4},{4,8},{8,12},{12,16},{16,20},{20,24},{24,28},{1,5},{5,9},{9,... | collective-permute-start | bytes 1572872 | tf_op jit(solution)/shard_map/ppermute | solution.py:21
  158.4 6.1 %collective-permute-done.x1 = f32[1,2,256,256]{3,2,1,0:T(8,128)S(1)} collective-permute-done((f32[1,2,256,256]{3,2,1,0:T(8,128)S(1)}, f32[1,2,256,256]{3,2,1,0:T(8,128)S(1)}, u32[]{:S(2)}, u32[]{:S(2)}) %collective-permute-start) | collective-permute-done | bytes 524320 | tf_op jit(solution)/shard_map/ppermute | solution.py:21
  168.9 6.1 %collective-permute-done.1.x2 = f32[1,2,256,256]{3,2,1,0:T(8,128)S(1)} collective-permute-done((f32[1,2,256,256]{3,2,1,0:T(8,128)S(1)}, f32[1,2,256,256]{3,2,1,0:T(8,128)S(1)}, u32[]{:S(2)}, u32[]{:S(2)}) %collective-permute-start.1) | collective-permute-done | bytes 524320 | tf_op jit(solution)/shard_map/ppermute | solution.py:21
  179.4 5.6 %copy.45 = f32[2,128,4096]{1,2,0:T(8,128)} copy(f32[2,128,4096]{2,1,0:T(8,128)} %param.13) | data formatting | bytes 8388608 | tf_op args[1]
  187.2 7.0 %spread.4 = f32[4,2,2,128,256]{4,3,2,1,0:T(8,128)} custom-call(f32[1,2,256,256]{3,2,1,0:T(8,128)S(1)} %get-tuple-element.11.x0, f32[1,2,256,256]{3,2,1,0:T(8,128)S(1)} %collective-permute-done.2.x3, f32[1,2,256,256]{3,2,1,0:T(8,128)S(1)} %collective-permute-done.1.x2, f32[1,2,256,256]{3,2,1,0:T(8,128)S(1)} %collective-permute-done.x1, ...), custom_call_target="tpu_custom_call" | custom-call | flops 3221225472 | bytes 4194304 | tf_op jit(solution)/shard_map/spread/pallas_call | solution.py:361
  195.2 4.6 all-to-all-start
  218.1 16.1 %fusion.1 = (f32[2,136,128,32]{2,3,1,0:T(8,128)S(1)}, f32[2,136,128,32]{2,3,1,0:T(8,128)S(1)}) fusion(f32[1,128,128,32]{2,3,1,0:T(8,128)S(1)} %broadcast_select_fusion, f32[1,128,128,32]{2,3,1,0:T(8,128)S(1)} %copy.52, f32[2,1,128,32]{2,3,1,0:T(8,128)S(1)} %maximum_bitcast_fusion), kind=kLoop, calls=%fused_computation.7 | loop fusion | flops 4456448 | bytes 13139968 | tf_op jit(solution)/shard_map/cos | solution.py:380
  238.3 12.1 %copy.53 = f32[17,2,2,32,8,128]{5,4,3,2,1,0:T(8,128)} copy(f32[17,2,2,32,8,128]{5,3,4,0,1,2:T(8,128)S(1)} %pad_maximum_fusion) | data formatting | bytes 17825792 | tf_op jit(solution)/shard_map/stack | solution.py:380
  250.4 6.2 %middle.7 = f32[4,2,2,32,1024]{4,3,2,1,0:T(8,128)S(1)} custom-call(s32[1]{0:T(128)} %bitcast.device, f32[4,2,2,128,256]{4,3,2,1,0:T(8,128)} %all-to-all-done.refs_0_, f32[4,2,2,128,256]{4,3,2,1,0:T(8,128)} %all-to-all-done.1.refs_1_, f32[4,2,2,128,256]{4,3,2,1,0:T(8,128)} %all-to-all-done.2.refs_2_, f32[4,2,2,128,256]{4,3,2,1,0:T(8,128)} %all-to-all-done.3.refs_3_, ...), custom_call_target="tpu_custom_call" | custom-call | flops 500000000 | bytes 6250000 | tf_op jit(solution)/shard_map/middle/pallas_call | solution.py:399
  262.5 5.9 %middle.6 = f32[4,2,2,32,1024]{4,3,2,1,0:T(8,128)S(1)} custom-call(s32[1]{0:T(128)} %bitcast.device, f32[4,2,2,128,256]{4,3,2,1,0:T(8,128)} %all-to-all-done.refs_0_, f32[4,2,2,128,256]{4,3,2,1,0:T(8,128)} %all-to-all-done.1.refs_1_, f32[4,2,2,128,256]{4,3,2,1,0:T(8,128)} %all-to-all-done.2.refs_2_, f32[4,2,2,128,256]{4,3,2,1,0:T(8,128)} %all-to-all-done.3.refs_3_, ...), custom_call_target="tpu_custom_call" | custom-call | flops 500000000 | bytes 6250000 | tf_op jit(solution)/shard_map/middle/pallas_call | solution.py:399
  269.7 40.5 %all-to-all-done.7.refs_3_ = f32[4,2,2,32,1024]{4,3,2,1,0:T(8,128)} async-done(((f32[4,2,2,32,1024]{4,3,2,1,0:T(8,128)}), f32[4,2,2,32,1024]{4,3,2,1,0:T(8,128)}, u32[]{:S(2)}, u32[]{:S(2)}) %all-to-all-start.7) | async-done | bytes 2097184 | tf_op jit(solution)/shard_map/all_to_all | solution.py:422
  314.7 5.9 %middle.5 = f32[4,2,2,32,1024]{4,3,2,1,0:T(8,128)S(1)} custom-call(s32[1]{0:T(128)} %bitcast.device, f32[4,2,2,128,256]{4,3,2,1,0:T(8,128)} %all-to-all-done.refs_0_, f32[4,2,2,128,256]{4,3,2,1,0:T(8,128)} %all-to-all-done.1.refs_1_, f32[4,2,2,128,256]{4,3,2,1,0:T(8,128)} %all-to-all-done.2.refs_2_, f32[4,2,2,128,256]{4,3,2,1,0:T(8,128)} %all-to-all-done.3.refs_3_, ...), custom_call_target="tpu_custom_call" | custom-call | flops 500000000 | bytes 6250000 | tf_op jit(solution)/shard_map/middle/pallas_call | solution.py:399
  322.0 40.4 %all-to-all-done.6.refs_2_ = f32[4,2,2,32,1024]{4,3,2,1,0:T(8,128)} async-done(((f32[4,2,2,32,1024]{4,3,2,1,0:T(8,128)}), f32[4,2,2,32,1024]{4,3,2,1,0:T(8,128)}, u32[]{:S(2)}, u32[]{:S(2)}) %all-to-all-start.6) | async-done | bytes 2097184 | tf_op jit(solution)/shard_map/all_to_all | solution.py:422
  366.9 7.4 %middle.4 = f32[4,2,2,32,1024]{4,3,2,1,0:T(8,128)S(1)} custom-call(s32[1]{0:T(128)} %bitcast.device, f32[4,2,2,128,256]{4,3,2,1,0:T(8,128)} %all-to-all-done.refs_0_, f32[4,2,2,128,256]{4,3,2,1,0:T(8,128)} %all-to-all-done.1.refs_1_, f32[4,2,2,128,256]{4,3,2,1,0:T(8,128)} %all-to-all-done.2.refs_2_, f32[4,2,2,128,256]{4,3,2,1,0:T(8,128)} %all-to-all-done.3.refs_3_, ...), custom_call_target="tpu_custom_call" | custom-call | flops 500000000 | bytes 6250000 | tf_op jit(solution)/shard_map/middle/pallas_call | solution.py:399
  375.6 39.0 %all-to-all-done.5.refs_1_ = f32[4,2,2,32,1024]{4,3,2,1,0:T(8,128)} async-done(((f32[4,2,2,32,1024]{4,3,2,1,0:T(8,128)}), f32[4,2,2,32,1024]{4,3,2,1,0:T(8,128)}, u32[]{:S(2)}, u32[]{:S(2)}) %all-to-all-start.5) | async-done | bytes 2097184 | tf_op jit(solution)/shard_map/all_to_all | solution.py:422
  414.6 51.7 %all_to_all.40.refs_0_ = f32[4,2,2,32,1024]{4,3,2,1,0:T(8,128)} all-to-all(f32[4,2,2,32,1024]{4,3,2,1,0:T(8,128)} %copy-done.3), channel_id=1, replica_groups=mesh['seg'=8,'fft'=4] {'fft'}, dimensions={0} | all-to-all | bytes 4194304 | tf_op jit(solution)/shard_map/all_to_all | solution.py:422
  466.3 9.0 %gather.1 = f32[1,2,256,1024]{3,2,1,0:T(8,128)} custom-call(f32[4,2,2,32,1024]{4,3,2,1,0:T(8,128)} %all_to_all.40.refs_0_, f32[4,2,2,32,1024]{4,3,2,1,0:T(8,128)} %all-to-all-done.5.refs_1_, f32[4,2,2,32,1024]{4,3,2,1,0:T(8,128)} %all-to-all-done.6.refs_2_, f32[4,2,2,32,1024]{4,3,2,1,0:T(8,128)} %all-to-all-done.7.refs_3_, ...), custom_call_target="tpu_custom_call" | custom-call | flops 3221225472 | bytes 20000000 | tf_op jit(solution)/shard_map/gather/pallas_call | solution.py:425
  (70 shorter events, 104.4 us)
Async XLA Ops:
  1.8 10.6 %collective-permute-start.9 = (f32[1,2,256,256]{3,2,1,0:T(8,128)S(1)}, f32[1,2,256,256]{3,2,1,0:T(8,128)S(1)}, u32[]{:S(2)}, u32[]{:S(2)}) collective-permute-start(f32[1,2,256,256]{3,2,1,0:T(8,128)S(1)} %get-tuple-element.9.x0), channel_id=1, source_target_pairs={{0,4},{4,8},{8,12},{12,16},{16,20},{20,24},{24,28},{1,5},{5,9},{9,... | collective-permute-start | bytes 1572872 | tf_op jit(solution)/shard_map/ppermute | solution.py:21
  12.4 10.5 %collective-permute-start.10 = (f32[1,2,256,256]{3,2,1,0:T(8,128)S(1)}, f32[1,2,256,256]{3,2,1,0:T(8,128)}, u32[]{:S(2)}, u32[]{:S(2)}) collective-permute-start(f32[1,2,256,256]{3,2,1,0:T(8,128)S(1)} %collective-permute-done.9.x1), channel_id=1, source_target_pairs={{0,4},{4,8},{8,12},{12,16},{16,20},{20,24},{24,28},{1,5},{5,9},{9,... | collective-permute-start | bytes 1572872 | tf_op jit(solution)/shard_map/ppermute | solution.py:21
  16.8 0.8 copy-start.10
  22.9 10.9 %collective-permute-start.11 = (f32[1,2,256,256]{3,2,1,0:T(8,128)}, f32[1,2,256,256]{3,2,1,0:T(8,128)}, u32[]{:S(2)}, u32[]{:S(2)}) collective-permute-start(f32[1,2,256,256]{3,2,1,0:T(8,128)} %collective-permute-done.10.x2), channel_id=1, source_target_pairs={{0,4},{4,8},{8,12},{12,16},{16,20},{20,24},{24,28},{1,5},{5,9},{9,... | collective-permute-start | bytes 1572872 | tf_op jit(solution)/shard_map/ppermute | solution.py:21
  33.8 1.0 copy-start.11
  42.4 47.3 %all-to-all-start.3 = ((f32[4,2,2,128,256]{4,3,2,1,0:T(8,128)}), f32[4,2,2,128,256]{4,3,2,1,0:T(8,128)}, u32[]{:S(2)}, u32[]{:S(2)}) async-start(f32[4,2,2,128,256]{4,3,2,1,0:T(8,128)} %spread.7), calls=%async_computation.3 | async-start | bytes 4194304 | tf_op jit(solution)/shard_map/all_to_all | solution.py:362
  46.9 10.8 %collective-permute-start.6 = (f32[1,2,256,256]{3,2,1,0:T(8,128)S(1)}, f32[1,2,256,256]{3,2,1,0:T(8,128)S(1)}, u32[]{:S(2)}, u32[]{:S(2)}) collective-permute-start(f32[1,2,256,256]{3,2,1,0:T(8,128)S(1)} %get-tuple-element.12.x0), channel_id=1, source_target_pairs={{0,4},{4,8},{8,12},{12,16},{16,20},{20,24},{24,28},{1,5},{5,9},{9,... | collective-permute-start | bytes 1572872 | tf_op jit(solution)/shard_map/ppermute | solution.py:21
  57.7 10.5 %collective-permute-start.7 = (f32[1,2,256,256]{3,2,1,0:T(8,128)S(1)}, f32[1,2,256,256]{3,2,1,0:T(8,128)S(1)}, u32[]{:S(2)}, u32[]{:S(2)}) collective-permute-start(f32[1,2,256,256]{3,2,1,0:T(8,128)S(1)} %collective-permute-done.6.x1), channel_id=1, source_target_pairs={{0,4},{4,8},{8,12},{12,16},{16,20},{20,24},{24,28},{1,5},{5,9},{9,... | collective-permute-start | bytes 1572872 | tf_op jit(solution)/shard_map/ppermute | solution.py:21
  68.2 10.5 %collective-permute-start.8 = (f32[1,2,256,256]{3,2,1,0:T(8,128)S(1)}, f32[1,2,256,256]{3,2,1,0:T(8,128)S(1)}, u32[]{:S(2)}, u32[]{:S(2)}) collective-permute-start(f32[1,2,256,256]{3,2,1,0:T(8,128)S(1)} %collective-permute-done.7.x2), channel_id=1, source_target_pairs={{0,4},{4,8},{8,12},{12,16},{16,20},{20,24},{24,28},{1,5},{5,9},{9,... | collective-permute-start | bytes 1572872 | tf_op jit(solution)/shard_map/ppermute | solution.py:21
  89.6 53.2 %all-to-all-start.2 = ((f32[4,2,2,128,256]{4,3,2,1,0:T(8,128)}), f32[4,2,2,128,256]{4,3,2,1,0:T(8,128)}, u32[]{:S(2)}, u32[]{:S(2)}) async-start(f32[4,2,2,128,256]{4,3,2,1,0:T(8,128)} %spread.6), calls=%async_computation.2 | async-start | bytes 4194304 | tf_op jit(solution)/shard_map/all_to_all | solution.py:362
  94.1 17.5 %collective-permute-start.3 = (f32[1,2,256,256]{3,2,1,0:T(8,128)S(1)}, f32[1,2,256,256]{3,2,1,0:T(8,128)S(1)}, u32[]{:S(2)}, u32[]{:S(2)}) collective-permute-start(f32[1,2,256,256]{3,2,1,0:T(8,128)S(1)} %get-tuple-element.10.x0), channel_id=1, source_target_pairs={{0,4},{4,8},{8,12},{12,16},{16,20},{20,24},{24,28},{1,5},{5,9},{9,... | collective-permute-start | bytes 1572872 | tf_op jit(solution)/shard_map/ppermute | solution.py:21
  111.6 10.5 %collective-permute-start.4 = (f32[1,2,256,256]{3,2,1,0:T(8,128)S(1)}, f32[1,2,256,256]{3,2,1,0:T(8,128)S(1)}, u32[]{:S(2)}, u32[]{:S(2)}) collective-permute-start(f32[1,2,256,256]{3,2,1,0:T(8,128)S(1)} %collective-permute-done.3.x1), channel_id=1, source_target_pairs={{0,4},{4,8},{8,12},{12,16},{16,20},{20,24},{24,28},{1,5},{5,9},{9,... | collective-permute-start | bytes 1572872 | tf_op jit(solution)/shard_map/ppermute | solution.py:21
  122.1 10.5 %collective-permute-start.5 = (f32[1,2,256,256]{3,2,1,0:T(8,128)S(1)}, f32[1,2,256,256]{3,2,1,0:T(8,128)S(1)}, u32[]{:S(2)}, u32[]{:S(2)}) collective-permute-start(f32[1,2,256,256]{3,2,1,0:T(8,128)S(1)} %collective-permute-done.4.x2), channel_id=1, source_target_pairs={{0,4},{4,8},{8,12},{12,16},{16,20},{20,24},{24,28},{1,5},{5,9},{9,... | collective-permute-start | bytes 1572872 | tf_op jit(solution)/shard_map/ppermute | solution.py:21
  142.8 52.4 %all-to-all-start.1 = ((f32[4,2,2,128,256]{4,3,2,1,0:T(8,128)}), f32[4,2,2,128,256]{4,3,2,1,0:T(8,128)}, u32[]{:S(2)}, u32[]{:S(2)}) async-start(f32[4,2,2,128,256]{4,3,2,1,0:T(8,128)} %spread.5), calls=%async_computation.1 | async-start | bytes 4194304 | tf_op jit(solution)/shard_map/all_to_all | solution.py:362
  147.3 17.2 %collective-permute-start = (f32[1,2,256,256]{3,2,1,0:T(8,128)S(1)}, f32[1,2,256,256]{3,2,1,0:T(8,128)S(1)}, u32[]{:S(2)}, u32[]{:S(2)}) collective-permute-start(f32[1,2,256,256]{3,2,1,0:T(8,128)S(1)} %get-tuple-element.11.x0), channel_id=1, source_target_pairs={{0,4},{4,8},{8,12},{12,16},{16,20},{20,24},{24,28},{1,5},{5,9},{9,... | collective-permute-start | bytes 1572872 | tf_op jit(solution)/shard_map/ppermute | solution.py:21
  164.5 10.5 %collective-permute-start.1 = (f32[1,2,256,256]{3,2,1,0:T(8,128)S(1)}, f32[1,2,256,256]{3,2,1,0:T(8,128)S(1)}, u32[]{:S(2)}, u32[]{:S(2)}) collective-permute-start(f32[1,2,256,256]{3,2,1,0:T(8,128)S(1)} %collective-permute-done.x1), channel_id=1, source_target_pairs={{0,4},{4,8},{8,12},{12,16},{16,20},{20,24},{24,28},{1,5},{5,9},{9,... | collective-permute-start | bytes 1572872 | tf_op jit(solution)/shard_map/ppermute | solution.py:21
  175.0 12.2 %collective-permute-start.2 = (f32[1,2,256,256]{3,2,1,0:T(8,128)S(1)}, f32[1,2,256,256]{3,2,1,0:T(8,128)S(1)}, u32[]{:S(2)}, u32[]{:S(2)}) collective-permute-start(f32[1,2,256,256]{3,2,1,0:T(8,128)S(1)} %collective-permute-done.1.x2), channel_id=1, source_target_pairs={{0,4},{4,8},{8,12},{12,16},{16,20},{20,24},{24,28},{1,5},{5,9},{9,... | collective-permute-start | bytes 1572872 | tf_op jit(solution)/shard_map/ppermute | solution.py:21
  195.2 55.3 %all-to-all-start = ((f32[4,2,2,128,256]{4,3,2,1,0:T(8,128)}), f32[4,2,2,128,256]{4,3,2,1,0:T(8,128)}, u32[]{:S(2)}, u32[]{:S(2)}) async-start(f32[4,2,2,128,256]{4,3,2,1,0:T(8,128)} %spread.4), calls=%async_computation | async-start | bytes 4194304 | tf_op jit(solution)/shard_map/all_to_all | solution.py:362
  238.2 12.2 %copy-start = (bf16[4,256,256]{2,1,0:T(8,128)(2,1)S(1)}, bf16[4,256,256]{2,1,0:T(8,128)(2,1)}, u32[]{:S(2)}) copy-start(bf16[4,256,256]{2,1,0:T(8,128)(2,1)} %constant.43.clone.refs_6_) | copy-start | bytes 1572868
  238.2 12.2 %copy-start.1 = (bf16[4,256,256]{2,1,0:T(8,128)(2,1)S(1)}, bf16[4,256,256]{2,1,0:T(8,128)(2,1)}, u32[]{:S(2)}) copy-start(bf16[4,256,256]{2,1,0:T(8,128)(2,1)} %constant.44.clone.refs_7_) | copy-start | bytes 1572868
  238.2 12.2 %copy-start.6 = (f32[2,2,32,128]{3,2,1,0:T(8,128)S(1)}, f32[2,2,32,128]{3,2,1,0:T(8,128)}, u32[]{:S(2)}) copy-start(f32[2,2,32,128]{3,2,1,0:T(8,128)} %constant.42.clone.refs_5_) | copy-start | bytes 196612
  238.3 12.2 %copy-start.7 = (f32[2,2,32,128]{3,2,1,0:T(8,128)S(1)}, f32[2,2,32,128]{3,2,1,0:T(8,128)}, u32[]{:S(2)}) copy-start(f32[2,2,32,128]{3,2,1,0:T(8,128)} %constant.45.clone.refs_8_) | copy-start | bytes 196612
  256.6 1.3 copy-start.5
  258.0 52.2 %all-to-all-start.7 = ((f32[4,2,2,32,1024]{4,3,2,1,0:T(8,128)}), f32[4,2,2,32,1024]{4,3,2,1,0:T(8,128)}, u32[]{:S(2)}, u32[]{:S(2)}) async-start(f32[4,2,2,32,1024]{4,3,2,1,0:T(8,128)} %copy-done.5), calls=%async_computation.7 | async-start | bytes 4194304 | tf_op jit(solution)/shard_map/all_to_all | solution.py:422
  268.4 1.3 copy-start.4
  310.2 52.2 %all-to-all-start.6 = ((f32[4,2,2,32,1024]{4,3,2,1,0:T(8,128)}), f32[4,2,2,32,1024]{4,3,2,1,0:T(8,128)}, u32[]{:S(2)}, u32[]{:S(2)}) async-start(f32[4,2,2,32,1024]{4,3,2,1,0:T(8,128)} %copy-done.4), calls=%async_computation.6 | async-start | bytes 4194304 | tf_op jit(solution)/shard_map/all_to_all | solution.py:422
  320.6 1.4 copy-start.2
  362.4 52.2 %all-to-all-start.5 = ((f32[4,2,2,32,1024]{4,3,2,1,0:T(8,128)}), f32[4,2,2,32,1024]{4,3,2,1,0:T(8,128)}, u32[]{:S(2)}, u32[]{:S(2)}) async-start(f32[4,2,2,32,1024]{4,3,2,1,0:T(8,128)} %copy-done.2), calls=%async_computation.5 | async-start | bytes 4194304 | tf_op jit(solution)/shard_map/all_to_all | solution.py:422
  374.3 1.3 copy-start.3
  375.6 90.7 %copy-start.8 = (bf16[256,1024]{1,0:T(8,128)(2,1)S(1)}, bf16[256,1024]{1,0:T(8,128)(2,1)}, u32[]{:S(2)}) copy-start(bf16[256,1024]{1,0:T(8,128)(2,1)} %constant.46.clone.refs_6_) | copy-start | bytes 1572868
  375.6 90.7 %copy-start.9 = (bf16[256,1024]{1,0:T(8,128)(2,1)S(1)}, bf16[256,1024]{1,0:T(8,128)(2,1)}, u32[]{:S(2)}) copy-start(bf16[256,1024]{1,0:T(8,128)(2,1)} %constant.47.clone.refs_7_) | copy-start | bytes 1572868

commit v2 on v0

v2 whole, which is shorter than its diff:
```python
import math

import jax
import jax.numpy as jnp
import ml_dtypes
import numpy as np
from jax import lax
from jax.experimental import pallas as pl
from jax.experimental.pallas import tpu as pltpu
from jax.sharding import PartitionSpec as P

LANES = 128
SUB = 8
VMEM = 50 * 1024 * 1024


def turn(products, period):
    angles = np.mod(products, period).astype(np.float64) * (-2.0 * math.pi / period)
    return np.cos(angles), np.sin(angles)


def halves(table):
    high = table.astype(ml_dtypes.bfloat16)
    low = (table - high.astype(np.float64)).astype(ml_dtypes.bfloat16)
    return high, low


def split(values):
    high = values.astype(jnp.bfloat16)
    low = (values - high.astype(jnp.float32)).astype(jnp.bfloat16)
    return high, low


def dot(left, right):
    return jnp.dot(left, right, preferred_element_type=jnp.float32)


def dot3(left_high, left_low, right_high, right_low):
    return dot(left_high, right_high) + (dot(left_high, right_low) + dot(left_low, right_high))


def scale_by(value, cos, sin):
    re, im = value
    near = 1e-12
    if abs(sin) < near:
        return value if cos > 0 else (-re, -im)
    if abs(cos) < near:
        return (-im, re) if sin > 0 else (im, -re)
    if abs(abs(cos) - abs(sin)) < near:
        size = abs(cos)
        first = re if cos > 0 else -re
        second = im if cos > 0 else -im
        third = im if sin > 0 else -im
        fourth = re if sin > 0 else -re
        return (first - third) * size, (second + fourth) * size
    return re * cos - im * sin, re * sin + im * cos


def plus(left, right):
    return left[0] + right[0], left[1] + right[1]


def minus(left, right):
    return left[0] - right[0], left[1] - right[1]


def small_dft(values, sign):
    count = len(values)
    if count == 1:
        return values
    if count == 2:
        return [plus(values[0], values[1]), minus(values[0], values[1])]
    if count == 4:
        even_sum, even_gap = plus(values[0], values[2]), minus(values[0], values[2])
        odd_sum, odd_gap = plus(values[1], values[3]), minus(values[1], values[3])
        turned = scale_by(odd_gap, 0.0, float(sign))
        return [plus(even_sum, odd_sum), plus(even_gap, turned), minus(even_sum, odd_sum), minus(even_gap, turned)]
    radix = 4 if count == 32 else 2
    part = count // radix
    pieces = [small_dft(values[i::radix], sign) for i in range(radix)]
    result = [None] * count
    for k in range(part):
        column = []
        for i in range(radix):
            angle = sign * 2.0 * math.pi * i * k / count
            column.append(scale_by(pieces[i][k], math.cos(angle), math.sin(angle)))
        for q, value in enumerate(small_dft(column, sign)):
            result[k + part * q] = value
    return result


def forward(value_at, twist, tab_high, tab_low, grid):
    spectra = []
    for parity in range(2):
        values = [value_at(parity, j) for j in range(twist.shape[2])]
        for k, (re, im) in enumerate(small_dft(values, -1)):
            w_re, w_im = twist[parity, 0, pl.ds(k, 1)], twist[parity, 1, pl.ds(k, 1)]
            grid[pl.ds(k * SUB, SUB), pl.ds(0, LANES)] = re * w_re - im * w_im
            grid[pl.ds(k * SUB, SUB), pl.ds(LANES, LANES)] = re * w_im + im * w_re
        high, low = split(grid[...])
        spectra.append(dot3(high, low, tab_high[parity], tab_low[parity]))
    even, odd = spectra
    return even + odd, even - odd


def backward(side_ref, parity, twist, tab_high, tab_low, grid, put):
    high, low = split(side_ref[parity])
    grid[...] = dot3(high, low, tab_high[2 + parity], tab_low[2 + parity])
    values = []
    for k in range(twist.shape[2]):
        re = grid[pl.ds(k * SUB, SUB), pl.ds(0, LANES)]
        im = grid[pl.ds(k * SUB, SUB), pl.ds(LANES, LANES)]
        w_re, w_im = twist[parity, 0, pl.ds(k, 1)], twist[parity, 1, pl.ds(k, 1)]
        values.append((re * w_re + im * w_im, im * w_re - re * w_im))
    for j, (re, im) in enumerate(small_dft(values, 1)):
        put(j, re, im)


def spread_kernel(x, table_high, table_low, turns, phases, out):
    count, slots, width = out.shape[0], out.shape[3], out.shape[4]
    first, second = zip(*(split(x[0, parity]) for parity in range(2)))
    high, low = jnp.concatenate(first, axis=1), jnp.concatenate(second, axis=1)
    sums = dot3(table_high[...], table_low[...], high, low).reshape(count, 2, slots, 2 * width)
    turn_re, turn_im = turns[:, 0], turns[:, 1]
    for parity in range(2):
        lanes = slice(parity * width, (parity + 1) * width)
        ph_re, ph_im = phases[:, 2 * parity], phases[:, 2 * parity + 1]
        re, im = sums[:, 0, :, lanes], sums[:, 1, :, lanes]
        w_re = turn_re * ph_re - turn_im * ph_im
        w_im = turn_re * ph_im + turn_im * ph_re
        out[:, parity, 0] = re * w_re - im * w_im
        out[:, parity, 1] = re * w_im + im * w_re


def chirp_kernel(position, chirp, twist, tab_high, tab_low, extra_turn, out, sides, grid, kept):
    step = pl.program_id(0)
    is_first = position[0] == 0
    on_extra = jnp.logical_and(is_first, step == 0)
    on_zero = jnp.logical_and(is_first, step == 1)
    points = twist.shape[2]

    @pl.when(jnp.logical_or(is_first, step > 0))
    def _():
        near_re, near_im, far_re, far_im = (chirp[0, n].reshape(points * SUB, LANES) for n in range(4))
        sides[0, :, pl.ds(0, LANES)] = near_re + far_re
        sides[0, :, pl.ds(LANES, LANES)] = near_im - far_im
        sides[1, :, pl.ds(0, LANES)] = near_re - far_re
        sides[1, :, pl.ds(LANES, LANES)] = near_im + far_im
        for parity in range(2):

            def put(j, re, im, parity=parity):
                out[j, parity, 0] = re
                out[j, parity, 1] = im

            backward(sides, parity, twist, tab_high, tab_low, grid, put)

    @pl.when(on_extra)
    def _():
        for parity in range(2):
            for j in range(points):
                w_re, w_im = extra_turn[parity, 0, pl.ds(j, 1)], extra_turn[parity, 1, pl.ds(j, 1)]
                kept[parity, j] = out[j, parity, 0] * w_re + out[j, parity, 1] * w_im

    @pl.when(on_zero)
    def _():
        keep = lax.broadcasted_iota(jnp.int32, (SUB, LANES), 0) > 0
        for parity in range(2):
            for j in range(points):
                out[j, parity, 1] = jnp.where(keep, out[j, parity, 1], kept[parity, j])


def response_kernel(
    parts, turns_in, phases_in, back_high, back_low, table_high, table_low, turns, phases, out, packed
):
    sources, slots = parts.shape[0], parts.shape[3]
    count, out_slots = out.shape[0], out.shape[4]
    for source in range(sources):
        t_re, t_im = turns_in[source, 0], turns_in[source, 1]
        for parity in range(2):
            ph_re, ph_im = phases_in[source, 2 * parity], phases_in[source, 2 * parity + 1]
            w_re = t_re * ph_re - t_im * ph_im
            w_im = t_re * ph_im + t_im * ph_re
            re, im = parts[source, parity, 0], parts[source, parity, 1]
            lanes = pl.ds(parity * LANES, LANES)
            for part, value in enumerate((re * w_re + im * w_im, im * w_re - re * w_im)):
                rows = pl.ds((2 * source + part) * slots, slots)
                packed[rows, lanes] = value
    first, second = split(packed[...])
    quarter = table_high.shape[1]
    for block in range(4):
        rows = pl.ds(block * quarter, quarter)
        taps = dot3(back_high[rows], back_low[rows], first, second)
        taps_high, taps_low = split(taps)
        sums = dot3(table_high[...], table_low[...], taps_high, taps_low)
        sums = sums.reshape(count, 2, out_slots, 2 * LANES)
        turn_re, turn_im = turns[:, 0], turns[:, 1]
        for parity in range(2):
            lanes = slice(parity * LANES, (parity + 1) * LANES)
            ph_re, ph_im = phases[:, 2 * parity], phases[:, 2 * parity + 1]
            re, im = sums[:, 0, :, lanes], sums[:, 1, :, lanes]
            w_re = turn_re * ph_re - turn_im * ph_im
            w_im = turn_re * ph_im + turn_im * ph_re
            out[:, block, parity, 0] = re * w_re - im * w_im
            out[:, block, parity, 1] = re * w_im + im * w_re


def forward_kernel(x, twist, tab_high, tab_low, out, grid):
    tiles = x.shape[5] // LANES

    def value_at(parity, j):
        group, tile = divmod(j, tiles)
        lanes = pl.ds(tile * LANES, LANES)
        return x[0, group, parity, 0, :, lanes], x[0, group, parity, 1, :, lanes]

    upper, lower = forward(value_at, twist, tab_high, tab_low, grid)
    out[0, 0] = upper
    out[0, 1] = lower


def apply_kernel(taps, spectrum, twist, tab_high, tab_low, out, response, ring, sides, grid):
    step = pl.program_id(0)
    points = twist.shape[2]
    tiles = out.shape[5] // LANES

    @pl.when(step < 4)
    def _():
        def value_at(parity, j):
            return taps[j, 0, parity, 0], taps[j, 0, parity, 1]

        upper, lower = forward(value_at, twist, tab_high, tab_low, grid)
        ring[step, 0] = upper
        ring[step, 1] = lower

    @pl.when(step == 3)
    def _():
        sign = 1.0 - 2.0 * (lax.broadcasted_iota(jnp.int32, (SUB, LANES), 0) % 2).astype(jnp.float32)
        re_lanes, im_lanes = pl.ds(0, LANES), pl.ds(LANES, LANES)
        for side in range(2):
            for k in range(points):
                rows = pl.ds(k * SUB, SUB)
                res = [ring[j, side, rows, re_lanes] for j in range(4)]
                ims = [ring[j, side, rows, im_lanes] for j in range(4)]
                for j in range(4):
                    response[j, side, rows, re_lanes] = res[j] - sign * ims[j - 1]
                    response[j, side, rows, im_lanes] = ims[j] + sign * res[j - 1]
        ring[...] = jnp.zeros_like(ring)

    @pl.when(step >= 4)
    def _():
        ring[lax.rem(step, 4)] = spectrum[0]
        slots = [lax.rem(step - j, 4) for j in range(4)]
        re_lanes, im_lanes = pl.ds(0, LANES), pl.ds(LANES, LANES)
        for k in range(points):
            rows = pl.ds(k * SUB, SUB)
            sums = []
            for side in range(2):
                total_re, total_im = 0.0, 0.0
                for j in range(4):
                    h_re, h_im = response[j, side, rows, re_lanes], response[j, side, rows, im_lanes]
                    x_re, x_im = ring[slots[j], side, rows, re_lanes], ring[slots[j], side, rows, im_lanes]
                    total_re += h_re * x_re - h_im * x_im
                    total_im += h_re * x_im + h_im * x_re
                sums.append((total_re, total_im))
            for parity, side in enumerate((plus(*sums), minus(*sums))):
                sides[parity, rows, re_lanes] = side[0]
                sides[parity, rows, im_lanes] = side[1]
        for parity in range(2):

            def put(j, re, im, parity=parity):
                group, tile = divmod(j, tiles)
                lanes = pl.ds(tile * LANES, LANES)
                out[0, group, parity, 0, :, lanes] = re
                out[0, group, parity, 1, :, lanes] = im

            backward(sides, parity, twist, tab_high, tab_low, grid, put)


def gather_kernel(parts, turns, phases, table_high, table_low, out):
    count, slots, width = parts.shape[0], parts.shape[3], parts.shape[4]
    turn_re, turn_im = turns[:, 0], turns[:, 1]
    columns = []
    for parity in range(2):
        ph_re, ph_im = phases[:, 2 * parity], phases[:, 2 * parity + 1]
        w_re = turn_re * ph_re - turn_im * ph_im
        w_im = turn_re * ph_im + turn_im * ph_re
        re, im = parts[:, parity, 0], parts[:, parity, 1]
        pair = jnp.stack([re * w_re + im * w_im, im * w_re - re * w_im], axis=1)
        columns.append(pair.reshape(count * 2 * slots, width))
    high, low = split(jnp.concatenate(columns, axis=1))
    sums = dot3(table_high[...], table_low[...], high, low)
    for parity in range(2):
        out[0, parity] = sums[:, parity * width : (parity + 1) * width]


def whole(shape):
    return pl.BlockSpec(shape, lambda i: (0,) * len(shape))


def call(kernel, name, grid, in_specs, out_specs, out_shape, scratch, flops, size):
    return pl.pallas_call(
        kernel,
        grid=(grid,),
        in_specs=in_specs,
        out_specs=out_specs,
        out_shape=jax.ShapeDtypeStruct(out_shape, jnp.float32),
        scratch_shapes=scratch,
        compiler_params=pltpu.CompilerParams(vmem_limit_bytes=VMEM, dimension_semantics=("arbitrary",)),
        cost_estimate=pl.CostEstimate(flops=int(flops), bytes_accessed=int(size), transcendentals=0),
        name=name,
    )


def exchange(values):
    return lax.all_to_all(values, ("seg", "fft"), split_axis=0, concat_axis=0, tiled=True)


def phase_pair(odd_rows, column, period):
    even = np.stack(turn(odd_rows * column, period), axis=-1)
    odd = np.stack(turn(odd_rows * (2 * column + 1), 2 * period), axis=-1)
    return np.concatenate([even, odd], axis=-1)


def per_device(voltage, chirp_phase):
    groups, segments = lax.axis_size("fft"), lax.axis_size("seg")
    group, segment = lax.axis_index("fft"), lax.axis_index("seg")
    count = groups * segments
    position = segment * groups + group
    quarter, width = voltage.shape[2], voltage.shape[3]
    row_count, half = 4 * quarter, 2 * quarter
    columns = width * groups
    points = columns // LANES
    total = row_count * columns
    short = total // 2
    slots = half // groups
    tile = min(2 * LANES, width // 4)
    f32 = jnp.float32

    keys, lanes = np.arange(points), np.arange(LANES)
    twist = np.stack(
        [
            np.stack(turn(keys[:, None] * lanes[None, :], columns)),
            np.stack(turn(keys[:, None] * (2 * lanes[None, :] + 1), 2 * columns)),
        ]
    ).astype(np.float32)
    tables = []
    for cos, sin in (
        turn(lanes[:, None] * lanes[None, :], LANES),
        turn((2 * lanes[:, None] + 1) * lanes[None, :], 2 * LANES),
    ):
        tables.append(np.block([[cos, sin], [-sin, cos]]))
    tab_high, tab_low = halves(np.stack(tables + [table.T for table in tables]))
    column_tables = [twist, tab_high, tab_low]
    column_specs = [whole(table.shape) for table in column_tables]

    own_rows = max(SUB, quarter // count)
    odd_rows = 2 * np.arange(own_rows * count) + 1
    live = (odd_rows < 2 * quarter).astype(np.float64)
    cos, sin = turn(odd_rows[:, None] * np.arange(quarter)[None, :], 2 * half)
    row_table = np.stack([cos, sin], axis=1) * live[:, None, None]
    row_table = row_table.reshape(count, own_rows, 2, quarter).transpose(0, 2, 1, 3).reshape(-1, quarter)
    row_high, row_low = halves(row_table)
    back_high, back_low = halves(row_table.T / short)
    turns = np.stack(turn(odd_rows[:, None] * np.arange(width)[None, :], 2 * short))
    turns = turns.reshape(2, count, own_rows, width).transpose(1, 0, 2, 3).astype(np.float32)

    def row_phases(column_starts):
        table = phase_pair(odd_rows[None, :], column_starts[:, None], 2 * short)
        table = table.reshape(-1, count, own_rows, 4).transpose(0, 1, 3, 2)
        return jnp.asarray(table[..., None].astype(np.float32))

    phases = lax.dynamic_index_in_dim(row_phases(np.arange(groups) * width), group, 0, keepdims=False)

    chirp_slots = max(SUB, slots // segments)
    holders = slots // chirp_slots
    blocks = chirp_slots // SUB
    is_first = position == 0
    start = jnp.minimum(segment, holders - 1) * chirp_slots
    own_phase = lax.dynamic_slice_in_dim(chirp_phase, start, chirp_slots, axis=1)
    digits = own_phase.reshape(2, chirp_slots, LANES, points)
    near, far = digits[0], digits[1, :, ::-1, ::-1]
    zero_row = jnp.roll(jnp.flip(own_phase[0, 0]), 1).reshape(LANES, points)
    at_zero = jnp.logical_and(is_first, jnp.arange(chirp_slots) == 0)[:, None, None]
    extra = jnp.pad(jnp.stack([digits[1, 0], far[0]])[:, None], ((0, 0), (0, SUB - 1), (0, 0), (0, 0)))
    far = jnp.where(at_zero, zero_row[None], far)
    angles = jnp.concatenate([extra, jnp.stack([near, far])], axis=1)
    angles = angles.reshape(2, blocks + 1, SUB, LANES, points).transpose(1, 0, 4, 2, 3)
    block, key, slot, lane = (lax.broadcasted_iota(jnp.int32, angles.shape, n) for n in (0, 2, 3, 4))
    dead = is_first & (block == 1) & (key == 0) & (slot == 0) & (lane == 0)
    dead = dead | (segment >= holders)
    chirp = jnp.stack([jnp.where(dead, 0.0, jnp.cos(angles)), jnp.where(dead, 0.0, jnp.sin(angles))], axis=2)
    chirp = chirp.reshape(blocks + 1, 4, points, SUB, LANES)
    every = LANES * keys[:, None] + lanes[None, :]
    extra_turn = np.stack(
        [np.stack(turn(half * every, total)), np.stack(turn(half * (2 * every + 1), 2 * total))]
    ).astype(np.float32)
    grid_scratch = pltpu.VMEM((points * SUB, 2 * LANES), f32)
    sides_scratch = pltpu.VMEM((2, points * SUB, 2 * LANES), f32)
    chirp_columns = call(
        chirp_kernel,
        "chirp_columns",
        blocks + 1,
        [pl.BlockSpec(memory_space=pltpu.SMEM), pl.BlockSpec((1, 4, points, SUB, LANES), lambda i: (i, 0, 0, 0, 0))]
        + column_specs
        + [whole(extra_turn.shape)],
        pl.BlockSpec((points, 2, 2, SUB, LANES), lambda i: (0, 0, 0, jnp.maximum(i - 1, 0), 0)),
        (points, 2, 2, chirp_slots, LANES),
        [sides_scratch, grid_scratch, pltpu.VMEM((2, points, SUB, LANES), f32)],
        2e8 * blocks,
        3e6,
    )(position.astype(jnp.int32).reshape(1), chirp, *column_tables, extra_turn)
    if count > points:
        chirp_columns = jnp.pad(chirp_columns, ((0, count - points),) + ((0, 0),) * 4)
    chirp_parts = exchange(chirp_columns)[: holders * groups]

    rows = np.arange(half)
    order = rows.reshape(groups, holders, chirp_slots).transpose(1, 0, 2)
    chirp_turns = np.stack(turn(order[..., None] * lanes, total), axis=2).astype(np.float32)
    block_of = np.arange(points)
    chirp_phases = phase_pair(order[None], LANES * block_of[:, None, None, None], total)
    chirp_phases = chirp_phases.reshape(points, holders * groups, chirp_slots, 4).transpose(0, 1, 3, 2)
    chirp_phases = jnp.asarray(chirp_phases[..., None].astype(np.float32))
    chirp_turns = chirp_turns.reshape(holders * groups, 2, chirp_slots, LANES)
    cos, sin = turn(rows[None, :] * np.arange(row_count)[:, None], row_count)
    cos[:, 0] = 0.5
    sin[:, 0] = np.where(np.arange(row_count) % 2 == 0, 0.5, -0.5)
    taps_table = np.stack([cos, sin], axis=1).reshape(row_count, 2, groups, holders, chirp_slots) / total
    taps_table = taps_table.transpose(0, 3, 2, 1, 4).reshape(row_count, 2 * half)
    taps_high, taps_low = halves(taps_table)
    own_block = jnp.minimum(position, points - 1)
    own_chirp_phases = lax.dynamic_index_in_dim(chirp_phases, own_block, 0, keepdims=False)
    own_row_phases = lax.dynamic_index_in_dim(row_phases(block_of * LANES), own_block, 0, keepdims=False)
    response_shape = (count, 4, 2, 2, own_rows, LANES)
    response = call(
        response_kernel,
        "response",
        1,
        [
            whole(chirp_parts.shape),
            whole(chirp_turns.shape),
            whole(own_chirp_phases.shape),
            whole(taps_high.shape),
            whole(taps_low.shape),
            whole(row_high.shape),
            whole(row_low.shape),
            pl.BlockSpec((count, 2, own_rows, LANES), lambda i: (0, 0, 0, 0)),
            whole(own_row_phases.shape),
        ],
        whole(response_shape),
        response_shape,
        [pltpu.VMEM((2 * half, 2 * LANES), f32)],
        5e9,
        1e7,
    )(chirp_parts, chirp_turns, own_chirp_phases, taps_high, taps_low, row_high, row_low, turns, own_row_phases)
    taps = exchange(response)[:points]

    spread_shape = (count, 2, 2, own_rows, width)
    spread = call(
        spread_kernel,
        "spread",
        width // tile,
        [
            pl.BlockSpec((1, 2, quarter, tile), lambda c: (0, 0, 0, c)),
            whole(row_high.shape),
            whole(row_low.shape),
            pl.BlockSpec((count, 2, own_rows, tile), lambda c: (0, 0, 0, c)),
            whole(phases.shape),
        ],
        pl.BlockSpec((count, 2, 2, own_rows, tile), lambda c: (0, 0, 0, 0, c)),
        spread_shape,
        [],
        2e9,
        1e7,
    )(voltage, row_high, row_low, turns, phases)
    spread = exchange(spread).reshape(segments, groups, 2, 2, own_rows, width)

    cells = (points * SUB, 2 * LANES)
    spectrum = call(
        forward_kernel,
        "forward",
        segments,
        [pl.BlockSpec((1, groups, 2, 2, own_rows, width), lambda s: (s, 0, 0, 0, 0, 0))] + column_specs,
        pl.BlockSpec((1, 2) + cells, lambda s: (s, 0, 0, 0)),
        (segments, 2) + cells,
        [grid_scratch],
        2e9,
        1e7,
    )(spread, *column_tables)

    def lagged(i):
        return jnp.maximum(i - 4, 0)

    packed = call(
        apply_kernel,
        "apply",
        segments + 4,
        [
            pl.BlockSpec((points, 1, 2, 2, own_rows, LANES), lambda i: (0, jnp.minimum(i, 3), 0, 0, 0, 0)),
            pl.BlockSpec((1, 2) + cells, lambda i: (lagged(i), 0, 0, 0)),
        ]
        + column_specs,
        pl.BlockSpec((1, groups, 2, 2, own_rows, width), lambda i: (lagged(i), 0, 0, 0, 0, 0)),
        (segments, groups, 2, 2, own_rows, width),
        [
            pltpu.VMEM((4, 2) + cells, f32),
            pltpu.VMEM((4, 2) + cells, f32),
            sides_scratch,
            grid_scratch,
        ],
        4e9,
        2e7,
    )(taps, spectrum, *column_tables)
    parts = exchange(packed.reshape(spread_shape))

    return call(
        gather_kernel,
        "gather",
        width // tile,
        [
            pl.BlockSpec((count, 2, 2, own_rows, tile), lambda c: (0, 0, 0, 0, c)),
            pl.BlockSpec((count, 2, own_rows, tile), lambda c: (0, 0, 0, c)),
            whole(phases.shape),
            whole(back_high.shape),
            whole(back_low.shape),
        ],
        pl.BlockSpec((1, 2, quarter, tile), lambda c: (0, 0, 0, c)),
        (1, 2, quarter, width),
        [],
        2e9,
        1e7,
    )(parts, turns, phases, back_high, back_low)


def solution(mesh):
    in_specs = (P("seg", None, None, "fft"), P(None, "fft", None))
    out_specs = P("seg", None, None, "fft")
    return jax.shard_map(per_device, mesh=mesh, in_specs=in_specs, out_specs=out_specs, check_vma=False)
```

time: 1210 us -> 316 us (0.26); the launches traced: 1190 us -> 315 us
  local copies, waits for them, and re-layouts: 428 us -> 17.8 us
  waiting for transfers between devices: 390 us -> 136 us
  other arithmetic: 216 us -> 3.35 us
  matrix products: 129 us -> 0 us
  blocking collectives: 0 us -> 97.3 us
  Pallas kernels: 0 us -> 44.3 us
    all_to_all x2 -> x3, waiting for transfers between devices: 322 us -> 136 us  [exchange(): lax.all_to_all(values, ('seg', 'fft'), split_axis=0, concat_axis=0, tiled...]
    rev x4 -> x1, local copies, waits for them, and re-layouts: 133 us -> 1.42 us  [per_device(): near, far = (digits[0], digits[1, :, ::-1, ::-1])]
    dot_general x6 -> x0, matrix products: 129 us -> none  [the longest x1 62.8 us: per_device(): jnp.einsum('pron,pqrm->qmon', lax.all_to_all(packed, 'fft', split_axis=2,...]
    slice x19 -> x9, local copies, waits for them, and re-layouts: 109 us -> 4.42 us  [the longest x2 2.2 us: per_device(): zero_row = jnp.roll(jnp.flip(own_phase[0, 0]), 1).reshape(LANES, points)]
    all_to_all x0 -> x1, blocking collectives: none -> 97.3 us  [exchange(): lax.all_to_all(values, ('seg', 'fft'), split_axis=0, concat_axis=0, tiled...]
    ppermute x3 -> x0, waiting for transfers between devices: 68.9 us -> none  [passed_along(): return lax.ppermute(shard, axis, pairs)]
    sub x6 -> x0, other arithmetic: 66 us -> none  [the longest x5 45.3 us: complex_mul(): first = left_pair[0] * right_pair[0] - left_pair[1] * right_pair[1]]
    scatter x4 -> x0, local copies, waits for them, and re-layouts: 45 us -> none  [the longest x2 22.5 us: mirrored(): flipped.at[:, half_count]]
  transfers between devices with their start and end apart: 5 -> 3, of which waited for: 5 -> 3; matrix products, arithmetic and copies ran while one was open for 4% -> 1% of each run, Pallas kernels for 0% -> 7%
where the time goes in v2:
time: 316 us; the launch traced here: 315 us
  waiting for transfers between devices  136 us (43%)
  blocking collectives  97.3 us (31%)
  Pallas kernels  44.3 us (14%)
  local copies, waits for them, and re-layouts  17.8 us (6%)
  starting transfers between devices  16.4 us (5%)
  other arithmetic  3.35 us (1%)
    all_to_all x3, waiting for transfers between devices, exchange(): lax.all_to_all(values, ('seg', 'fft'), split_axis=0, concat_axis=0, tiled...  136 us
    all_to_all x1, blocking collectives, exchange(): lax.all_to_all(values, ('seg', 'fft'), split_axis=0, concat_axis=0, tiled...  97.3 us
    all_to_all x3, starting transfers between devices, exchange(): lax.all_to_all(values, ('seg', 'fft'), split_axis=0, concat_axis=0, tiled...  16.4 us
    pallas_call x1, Pallas kernels, per_device(): call(apply_kernel, 'apply', segments + 4, [pl.BlockSpec((points, 1, 2, 2,...  12.9 us
    pallas_call x1, Pallas kernels, per_device(): call(response_kernel, 'response', 1, [whole(chirp_parts.shape), whole(chi...  9.47 us
    pallas_call x1, Pallas kernels, per_device(): call(forward_kernel, 'forward', segments, [pl.BlockSpec((1, groups, 2, 2,...  8.5 us
  transfers between devices with their start and end apart: 3, of which 3 were waited for; matrix products, arithmetic and copies ran while one was open for 1% of the time, Pallas kernels for 7%

profile of v2, /device:TPU:1, one launch (start us, length us, event | category | flops | bytes accessed | tf_op | source)
XLA Modules:
  0.0 315.0 jit_solution(3968758228147477050)
XLA Ops:
  0.1 1.2 constant_dynamic-slice_fusion.1
  1.3 1.0 constant_dynamic-slice_fusion
  2.3 1.1 constant_dynamic-slice_fusion.2
  3.3 1.1 constant_dynamic-slice_fusion.4
  4.8 1.4 rev.5
  6.4 0.7 pad_maximum_fusion.1
  8.5 0.7 reshape.30
  9.3 2.0 fusion.1
  11.8 1.1 copy.32
  12.9 1.9 chirp_columns.1
  14.9 7.1 %all-to-all-start = ((f32[32,2,2,16,128]{4,3,2,1,0:T(8,128)}), f32[32,2,2,16,128]{4,3,2,1,0:T(8,128)}, u32[]{:S(2)}, u32[]{:S(2)}) async-start(f32[32,2,2,16,128]{4,3,2,1,0:T(8,128)} %chirp_columns.1), calls=%async_computation | async-start | bytes 2097152 | tf_op jit(solution)/shard_map/all_to_all | solution.py:314
  22.0 0.7 dynamic-slice_bitcast_fusion.1
  22.8 0.5 copy.35.phases
  23.3 0.9 copy-done.10
  24.3 5.5 %spread.1 = f32[32,2,2,8,1024]{4,3,2,1,0:T(8,128)} custom-call(f32[1,2,256,1024]{3,2,1,0:T(8,128)S(1)} %copy-done.5, bf16[512,256]{1,0:T(8,128)(2,1)S(1)} %copy-done.10, bf16[512,256]{1,0:T(8,128)(2,1)S(1)} %copy-done.9, f32[32,2,8,1024]{3,2,1,0:T(8,128)} %constant.85.clone.turns, f32[32,4,8,1]{3,2,1,0:T(8,128)S(1)} %copy.35.phases), custom_call_target="tpu_custom_call" | custom-call | flops 2000000000 | bytes 10000000 | tf_op jit(solution)/shard_map/spread/pallas_call | solution.py:457
  29.8 18.7 %all-to-all-done.parts = f32[32,2,2,16,128]{4,3,2,1,0:T(8,128)} async-done(((f32[32,2,2,16,128]{4,3,2,1,0:T(8,128)}), f32[32,2,2,16,128]{4,3,2,1,0:T(8,128)}, u32[]{:S(2)}, u32[]{:S(2)}) %all-to-all-start) | async-done | bytes 1048608 | tf_op jit(solution)/shard_map/all_to_all | solution.py:314
  48.4 3.3 %all-to-all-start.2 = ((f32[32,2,2,8,1024]{4,3,2,1,0:T(8,128)}), f32[32,2,2,8,1024]{4,3,2,1,0:T(8,128)}, u32[]{:S(2)}, u32[]{:S(2)}) async-start(f32[32,2,2,8,1024]{4,3,2,1,0:T(8,128)} %spread.1), calls=%async_computation.2 | async-start | bytes 8388608 | tf_op jit(solution)/shard_map/all_to_all | solution.py:314
  51.8 0.7 dynamic-slice_bitcast_fusion.2
  52.5 0.5 copy.34.phases
  53.0 0.8 dynamic-slice_bitcast_fusion
  53.8 1.0 copy.33.phases_in
  54.8 1.0 copy-done.13
  55.9 9.5 %response.1 = f32[32,4,2,2,8,128]{5,4,3,2,1,0:T(8,128)} custom-call(f32[32,2,2,16,128]{4,3,2,1,0:T(8,128)} %all-to-all-done.parts, f32[32,2,16,128]{3,2,1,0:T(8,128)S(1)} %copy-done.13, f32[32,4,16,1]{3,2,1,0:T(8,128)S(1)} %copy.33.phases_in, bf16[1024,1024]{1,0:T(8,128)(2,1)} %constant.81.clone.back_high, bf16[1024,1024]{1,0:T(8,128)(2,1)} %constant.82.clone.back_low, ...), custom_call_target="tpu_custom_call" | custom-call | flops 5000000000 | bytes 10000000 | tf_op jit(solution)/shard_map/response/pallas_call | solution.py:433
  65.3 78.3 %all-to-all-done.2 = f32[32,2,2,8,1024]{4,3,2,1,0:T(8,128)} async-done(((f32[32,2,2,8,1024]{4,3,2,1,0:T(8,128)}), f32[32,2,2,8,1024]{4,3,2,1,0:T(8,128)}, u32[]{:S(2)}, u32[]{:S(2)}) %all-to-all-start.2) | async-done | bytes 4194336 | tf_op jit(solution)/shard_map/all_to_all | solution.py:314
  143.6 5.9 %all-to-all-start.1 = ((f32[32,4,2,2,8,128]{5,4,3,2,1,0:T(8,128)}), f32[32,4,2,2,8,128]{5,4,3,2,1,0:T(8,128)S(1)}, u32[]{:S(2)}, u32[]{:S(2)}) async-start(f32[32,4,2,2,8,128]{5,4,3,2,1,0:T(8,128)} %response.1), calls=%async_computation.1 | async-start | bytes 4194304 | tf_op jit(solution)/shard_map/all_to_all | solution.py:314
  149.6 1.0 copy-done.3
  150.6 8.5 %forward.1.spectrum = f32[8,2,256,256]{3,2,1,0:T(8,128)} custom-call(f32[8,4,2,2,8,1024]{5,4,3,2,1,0:T(8,128)} %bitcast.16.x, f32[2,2,32,128]{3,2,1,0:T(8,128)S(1)} %copy-done.6, bf16[4,256,256]{2,1,0:T(8,128)(2,1)S(1)} %copy-done.3, bf16[4,256,256]{2,1,0:T(8,128)(2,1)S(1)} %copy-done.1), custom_call_target="tpu_custom_call" | custom-call | flops 2000000000 | bytes 10000000 | tf_op jit(solution)/shard_map/forward/pallas_call | solution.py:477
  159.1 38.7 %all-to-all-done.1.taps = f32[32,4,2,2,8,128]{5,4,3,2,1,0:T(8,128)S(1)} async-done(((f32[32,4,2,2,8,128]{5,4,3,2,1,0:T(8,128)}), f32[32,4,2,2,8,128]{5,4,3,2,1,0:T(8,128)S(1)}, u32[]{:S(2)}, u32[]{:S(2)}) %all-to-all-start.1) | async-done | bytes 2097184 | tf_op jit(solution)/shard_map/all_to_all | solution.py:314
  197.8 1.0 copy-done.4
  198.8 12.9 %apply.1 = f32[8,4,2,2,8,1024]{5,4,3,2,1,0:T(8,128)} custom-call(f32[32,4,2,2,8,128]{5,4,3,2,1,0:T(8,128)S(1)} %all-to-all-done.1.taps, f32[8,2,256,256]{3,2,1,0:T(8,128)} %forward.1.spectrum, f32[2,2,32,128]{3,2,1,0:T(8,128)S(1)} %copy-done.6, bf16[4,256,256]{2,1,0:T(8,128)(2,1)S(1)} %copy-done.4, bf16[4,256,256]{2,1,0:T(8,128)(2,1)S(1)} %copy-done.1), custom_call_target="tpu_custom_call" | custom-call | flops 4000000000 | bytes 20000000 | tf_op jit(solution)/shard_map/apply/pallas_call | solution.py:492
  211.7 97.3 %all_to_all.20.parts = f32[32,2,2,8,1024]{4,3,2,1,0:T(8,128)} all-to-all(f32[32,2,2,8,1024]{4,3,2,1,0:T(8,128)} %bitcast.31), channel_id=1, replica_groups=mesh['seg'=8,'fft'=4] {'seg','fft'}, dimensions={0} | all-to-all | bytes 8388608 | tf_op jit(solution)/shard_map/all_to_all | solution.py:314
  309.0 6.1 %gather.1 = f32[1,2,256,1024]{3,2,1,0:T(8,128)} custom-call(f32[32,2,2,8,1024]{4,3,2,1,0:T(8,128)} %all_to_all.20.parts, f32[32,2,8,1024]{3,2,1,0:T(8,128)S(1)} %copy-done, f32[32,4,8,1]{3,2,1,0:T(8,128)S(1)} %copy.35.phases, bf16[256,512]{1,0:T(8,128)(2,1)S(1)} %copy-done.8, bf16[256,512]{1,0:T(8,128)(2,1)S(1)} %copy-done.7), custom_call_target="tpu_custom_call" | custom-call | flops 2000000000 | bytes 10000000 | tf_op jit(solution)/shard_map/gather/pallas_call | solution.py:514
  (45 shorter events, 2.5 us)
Async XLA Ops:
  11.7 1.2 copy-start.1
  11.7 1.2 copy-start.2
  11.7 1.2 copy-start.6
  11.8 1.2 copy-start.12
  14.9 8.4 %copy-start.5 = (f32[1,2,256,1024]{3,2,1,0:T(8,128)S(1)}, f32[1,2,256,1024]{3,2,1,0:T(8,128)}, u32[]{:S(2)}) copy-start(f32[1,2,256,1024]{3,2,1,0:T(8,128)} %x.3) | copy-start | bytes 6291460
  14.9 8.4 %copy-start.9 = (bf16[512,256]{1,0:T(8,128)(2,1)S(1)}, bf16[512,256]{1,0:T(8,128)(2,1)}, u32[]{:S(2)}) copy-start(bf16[512,256]{1,0:T(8,128)(2,1)} %constant.84.clone.table_low) | copy-start | bytes 786436
  14.9 33.6 %all-to-all-start = ((f32[32,2,2,16,128]{4,3,2,1,0:T(8,128)}), f32[32,2,2,16,128]{4,3,2,1,0:T(8,128)}, u32[]{:S(2)}, u32[]{:S(2)}) async-start(f32[32,2,2,16,128]{4,3,2,1,0:T(8,128)} %chirp_columns.1), calls=%async_computation | async-start | bytes 2097152 | tf_op jit(solution)/shard_map/all_to_all | solution.py:314
  23.3 1.0 copy-start.10
  29.8 25.1 %copy-start.11 = (bf16[512,256]{1,0:T(8,128)(2,1)S(1)}, bf16[512,256]{1,0:T(8,128)(2,1)}, u32[]{:S(2)}) copy-start(bf16[512,256]{1,0:T(8,128)(2,1)} %constant.83.clone.table_high) | copy-start | bytes 786436
  48.4 95.2 %all-to-all-start.2 = ((f32[32,2,2,8,1024]{4,3,2,1,0:T(8,128)}), f32[32,2,2,8,1024]{4,3,2,1,0:T(8,128)}, u32[]{:S(2)}, u32[]{:S(2)}) async-start(f32[32,2,2,8,1024]{4,3,2,1,0:T(8,128)} %spread.1), calls=%async_computation.2 | async-start | bytes 8388608 | tf_op jit(solution)/shard_map/all_to_all | solution.py:314
  54.8 1.0 copy-start.13
  143.6 54.2 %all-to-all-start.1 = ((f32[32,4,2,2,8,128]{5,4,3,2,1,0:T(8,128)}), f32[32,4,2,2,8,128]{5,4,3,2,1,0:T(8,128)S(1)}, u32[]{:S(2)}, u32[]{:S(2)}) async-start(f32[32,4,2,2,8,128]{5,4,3,2,1,0:T(8,128)} %response.1), calls=%async_computation.1 | async-start | bytes 4194304 | tf_op jit(solution)/shard_map/all_to_all | solution.py:314
  149.5 1.0 copy-start.3
  197.8 1.0 copy-start.4
  211.7 97.3 %copy-start = (f32[32,2,8,1024]{3,2,1,0:T(8,128)S(1)}, f32[32,2,8,1024]{3,2,1,0:T(8,128)}, u32[]{:S(2)}) copy-start(f32[32,2,8,1024]{3,2,1,0:T(8,128)} %constant.85.clone.turns) | copy-start | bytes 6291460
  211.7 97.3 %copy-start.7 = (bf16[256,512]{1,0:T(8,128)(2,1)S(1)}, bf16[256,512]{1,0:T(8,128)(2,1)}, u32[]{:S(2)}) copy-start(bf16[256,512]{1,0:T(8,128)(2,1)} %constant.87.clone.table_low) | copy-start | bytes 786436
  211.7 97.3 %copy-start.8 = (bf16[256,512]{1,0:T(8,128)(2,1)S(1)}, bf16[256,512]{1,0:T(8,128)(2,1)}, u32[]{:S(2)}) copy-start(bf16[256,512]{1,0:T(8,128)(2,1)} %constant.86.clone.table_high) | copy-start | bytes 786436
